TPU v7x, 512 devices: a whole 4x8x8 slice. The times are simulated.
512 devices in a mesh: rows: 128 (over z, y, core), cols: 4 (over x).
Axes of the slice: x: 4, y: 8, z: 8, core: 2. Of those that a mesh axis runs over, the one named last changes fastest.
Arguments:
- matrix: float32 [262144, 512], P('rows', 'cols'), may hold values from -140 to 140, as said below
- order: int32 [2, 256], replicated, may hold values from 0 to 255, each once within a row
Outputs:
- density: float32 [262144, 512], P('rows', 'cols')
- col_rms: float32 [512], P('cols')
Inputs may be any that keep to these rules, and one draw needn't show every extreme that they name: Each row of order is a permutation of 0 .. 255. `matrix`: entries are real numbers of order one to some tens.
All inputs are finite; a program needn't handle non-finite values.
Results may differ from a plain program's by a relative error of at most 0.0003.
Values sent between devices are 32-bit elements; how exact they have to be, the bound alone decides.
No kernel may reach another device: no remote copies, remote signals or barrier semaphores. Data moves between devices by JAX's collectives and lax.ppermute only.
A program may use at most 64 MiB of HBM per device.

v0:
```python
import jax
import jax.numpy as jnp
from jax import lax
from jax.sharding import PartitionSpec as P

ROUNDS = 16


eps = 1e-06


def partner_2(block, axis, distance):
    count = lax.axis_size(axis)
    route = []
    for low in range(count):
        high = low | 1 << distance
        if high != low and high < count:
            route += [(low, high), (high, low)]
    return lax.ppermute(block, axis, route)


def exact_dot(left, right):
    return jnp.dot(left, right, precision=lax.Precision.HIGHEST, preferred_element_type=jnp.float32)


def rotate_pairs(gram, order_row, round_count):
    order_size = gram.shape[0]
    half_size = order_size // 2
    last_slot = order_size - 1
    basis_start = jnp.eye(order_size, dtype=gram.dtype)
    column_ids = jnp.arange(order_size, dtype=jnp.int32)

    def one_round(round_index, state_pair):
        turned, rotation_basis = state_pair
        round_now = jnp.asarray(round_index).astype(jnp.int32)
        slot_index = jnp.arange(half_size, dtype=jnp.int32)
        left_slot = jnp.where(slot_index == 0, last_slot, (round_now + slot_index) % last_slot)
        right_slot = (round_now - slot_index) % last_slot
        col_left = order_row[left_slot]
        col_right = order_row[right_slot]
        diag_left = turned[col_left, col_left]
        diag_right = turned[col_right, col_right]
        cross_term = turned[col_left, col_right]
        rot_angle = 0.5 * jnp.arctan2(2.0 * cross_term, diag_right - diag_left)
        cosine = jnp.cos(rot_angle)[:, None]
        sine_part = jnp.sin(rot_angle)[:, None]
        onehot_left = (col_left[:, None] == column_ids[None, :]).astype(jnp.float32)
        onehot_right = (col_right[:, None] == column_ids[None, :]).astype(jnp.float32)
        stacked = jnp.concatenate([onehot_left, onehot_right], axis=0)
        weights = jnp.concatenate(
            [
                cosine * onehot_left + sine_part * onehot_right,
                cosine * onehot_right - sine_part * onehot_left,
            ],
            axis=0,
        )
        rotation = exact_dot(stacked.T, weights)
        turned = exact_dot(rotation.T, exact_dot(turned, rotation))
        rotation_basis = exact_dot(rotation_basis, rotation)
        return (turned, rotation_basis)

    return lax.fori_loop(0, round_count, one_round, (gram, basis_start))


def pair_gram(joined):
    return exact_dot(joined.T, joined)


def local(matrix, order):
    current = matrix
    local_rows = current.shape[0]
    block_width = current.shape[1]
    col_count = lax.axis_size("cols")
    far_bit = col_count.bit_length() - 2
    keep_start = None
    for tourney_step, swap_bit in enumerate((0, far_bit)):
        lower_flag = lax.axis_index("cols") >> swap_bit & 1 == 0
        partner = partner_2(current, "cols", swap_bit)
        joined = jnp.concatenate(
            [jnp.where(lower_flag, current, partner), jnp.where(lower_flag, partner, current)],
            axis=1,
        )
        partial_value = pair_gram(joined)
        gram_total = lax.psum(partial_value, "rows")
        turned, rotation_basis = rotate_pairs(gram_total, order[tourney_step], ROUNDS)
        keep_start = jnp.where(lower_flag, 0, block_width).astype(jnp.int32)
        kept_basis = lax.dynamic_slice_in_dim(rotation_basis, keep_start, block_width, 1)
        current = exact_dot(joined, kept_basis)
    density = current * current
    row_total = local_rows * lax.axis_size("rows")
    squares_sum = lax.psum(jnp.sum(density, axis=0), "rows")
    col_rms = jnp.sqrt(squares_sum / row_total + eps)
    return (density, col_rms)


def solution(mesh):
    placed = (P("rows", "cols"), P())
    return jax.shard_map(
        local, mesh=mesh, in_specs=placed, out_specs=(P("rows", "cols"), P("cols")), check_vma=False
    )
```

profile of v0, /device:TPU:1, one launch (start us, length us, event | category | flops | bytes accessed | tf_op | source)
XLA Modules:
  0.0 1050.9 jit_solution(14347701195405672576)
XLA Ops:
  7.2 4.0 collective-permute-start
  11.2 18.1 %collective-permute-done = f32[2048,128]{1,0:T(8,128)} collective-permute-done((f32[2048,128]{1,0:T(8,128)}, f32[2048,128]{1,0:T(8,128)}, u32[]{:S(2)}, u32[]{:S(2)}) %collective-permute-start) | collective-permute-done | bytes 1048608 | tf_op jit(solution)/shard_map/ppermute | solution.py:19
  29.3 1.7 broadcast_select_fusion.1
  31.1 4.3 fusion.32
  35.5 199.3 %all-reduce.3.cloned.1.call-done = f32[256,256]{1,0:T(8,128)} async-done(((f32[256,256]{1,0:T(8,128)}), f32[256,256]{1,0:T(8,128)}) %all-reduce.3.cloned.1.call-update) | async-done | bytes 262160 | tf_op jit(solution)/shard_map/psum | solution.py:84
  234.8 167.1 %while.38 = (s32[]{:T(128)}, f32[256,256]{1,0:T(8,128)}, f32[256,256]{0,1:T(8,128)S(1)}, s32[256]{0:T(256)S(1)}, s32[]{:T(128)}) while((s32[]{:T(128)}, f32[256,256]{1,0:T(8,128)}, f32[256,256]{0,1:T(8,128)S(1)}, s32[256]{0:T(256)S(1)}, s32[]{:T(128)}) %tuple.126), condition=%wide.region_2.3_spmd.clone.clone, body=%wide.region_1.2_spmd.clone.clone.sunk | while | flops 805772288 | bytes 4878429 | solution.py:62
  237.4 1.5 gather_fusion.2
  240.4 1.5 gather_fusion.4
  247.9 1.5 gather_fusion.2
  249.3 1.5 gather_fusion.3
  250.8 1.5 gather_fusion.4
  258.3 1.5 gather_fusion.2
  259.8 1.5 gather_fusion.3
  261.3 1.5 gather_fusion.4
  268.7 1.5 gather_fusion.2
  401.9 3.3 fusion.31
  405.1 4.8 collective-permute-start.1
  409.9 22.0 %collective-permute-done.1 = f32[2048,128]{0,1:T(8,128)} collective-permute-done((f32[2048,128]{0,1:T(8,128)}, f32[2048,128]{0,1:T(8,128)}, u32[]{:S(2)}, u32[]{:S(2)}) %collective-permute-start.1) | collective-permute-done | bytes 1048608 | tf_op jit(solution)/shard_map/ppermute | solution.py:19
  431.9 1.8 broadcast_select_fusion.3
  433.7 2.6 fusion.30
  436.3 188.1 %all-reduce.5.cloned.1.call-done = f32[256,256]{1,0:T(8,128)} async-done(((f32[256,256]{1,0:T(8,128)}), f32[256,256]{1,0:T(8,128)}) %all-reduce.5.cloned.1.call-update) | async-done | bytes 262160 | tf_op jit(solution)/shard_map/psum | solution.py:84
  624.4 167.0 %while.39 = (s32[]{:T(128)}, f32[256,256]{1,0:T(8,128)}, f32[256,256]{0,1:T(8,128)S(1)}, s32[256]{0:T(256)S(1)}, s32[]{:T(128)}) while((s32[]{:T(128)}, f32[256,256]{1,0:T(8,128)}, f32[256,256]{0,1:T(8,128)S(1)}, s32[256]{0:T(256)S(1)}, s32[]{:T(128)}) %tuple.125), condition=%wide.region_5.6_spmd.clone.clone, body=%wide.region_4.5_spmd.clone.clone.sunk | while | flops 805772288 | bytes 4878429 | solution.py:62
  791.4 4.4 fusion.45
  795.8 247.7 %psum.23 = f32[128]{0:T(128)S(1)} all-reduce(f32[128]{0:T(128)S(1)} %get-tuple-element.364), channel_id=1, replica_groups=mesh['rows'=128,'cols'=4] {'rows'}, use_global_device_ids=true, to_apply=%region_7.8 | all-reduce | flops 128 | bytes 1024 | tf_op jit(solution)/shard_map/psum | solution.py:91
  (678 shorter events, 317.3 us)
Async XLA Ops:
  7.2 227.6 %all-reduce.3.cloned.1.call-start = ((), (), s32[]{:S(2)}) async-start(), calls=%async_computation | async-start | bytes 524288 | tf_op jit(solution)/shard_map/psum | solution.py:84
  7.2 22.1 %collective-permute-start = (f32[2048,128]{1,0:T(8,128)}, f32[2048,128]{1,0:T(8,128)}, u32[]{:S(2)}, u32[]{:S(2)}) collective-permute-start(f32[2048,128]{1,0:T(8,128)} %param.6), channel_id=1, source_target_pairs={{0,1},{1,0},{2,3},{3,2},{4,5},{5,4},{6,7},{7,6},{8,9},{9,8},{10,11... | collective-permute-start | bytes 3145736 | tf_op jit(solution)/shard_map/ppermute | solution.py:19
  11.2 19.8 %copy-start.2 = (f32[256,256]{0,1:T(8,128)}, f32[256,256]{0,1:T(8,128)S(1)}, u32[]{:S(2)}) copy-start(f32[256,256]{0,1:T(8,128)S(1)} %fusion.33) | copy-start | bytes 786436
  31.0 4.4 copy-start.5
  31.1 203.7 %copy-start.4 = (f32[256,256]{0,1:T(8,128)S(1)}, f32[256,256]{0,1:T(8,128)}, u32[]{:S(2)}) copy-start(f32[256,256]{0,1:T(8,128)} %copy-done.2) | copy-start | bytes 786436
  35.4 589.0 %all-reduce.5.cloned.1.call-start = ((), (), s32[]{:S(2)}) async-start(), calls=%async_computation.1 | async-start | bytes 524288 | tf_op jit(solution)/shard_map/psum | solution.py:84
  234.8 2.6 copy-start
  245.2 2.6 copy-start
  255.7 2.6 copy-start
  266.1 2.6 copy-start
  276.6 2.6 copy-start
  287.0 2.6 copy-start
  297.5 2.6 copy-start
  307.9 2.6 copy-start
  318.3 2.6 copy-start
  328.8 2.6 copy-start
  339.2 2.6 copy-start
  349.7 2.6 copy-start
  360.1 2.6 copy-start
  370.5 2.6 copy-start
  381.0 2.6 copy-start
  405.1 26.8 %collective-permute-start.1 = (f32[2048,128]{0,1:T(8,128)}, f32[2048,128]{0,1:T(8,128)}, u32[]{:S(2)}, u32[]{:S(2)}) collective-permute-start(f32[2048,128]{0,1:T(8,128)} %fusion.31), channel_id=1, source_target_pairs={{0,2},{2,0},{1,3},{3,1},{4,6},{6,4},{5,7},{7,5},{8,10},{10,8},{9,1... | collective-permute-start | bytes 3145736 | tf_op jit(solution)/shard_map/ppermute | solution.py:19
  433.7 190.7 %copy-start.3 = (f32[256,256]{0,1:T(8,128)S(1)}, f32[256,256]{0,1:T(8,128)}, u32[]{:S(2)}) copy-start(f32[256,256]{0,1:T(8,128)} %copy-done.2) | copy-start | bytes 786436
  624.4 2.6 copy-start.1
  (16 other events, 41.8 us)
Sparse Core Ops, SparseCore 0:
  35.5 199.2 all-reduce.2
  436.4 187.9 all-reduce.4
where the time goes:
time: 1050 us
  waiting for transfers between devices  428 us (41%)
  blocking collectives  248 us (24%)
  local copies, waits for them, and re-layouts  224 us (21%)
  matrix products  107 us (10%)
  other arithmetic  17.6 us (2%)
  between operations  14.2 us (1%)
    psum x2, waiting for transfers between devices, local(): gram_total = lax.psum(partial_value, 'rows')  387 us
    psum x1, blocking collectives, local(): squares_sum = lax.psum(jnp.sum(density, axis=0), 'rows')  248 us
    dot_general x132, matrix products, exact_dot(): jnp.dot(left, right, precision=lax.Precision.HIGHEST, preferred_element_t...  107 us
    gather x32, local copies, waits for them, and re-layouts, one_round(): diag_right = turned[col_right, col_right]  47.1 us
    gather x32, local copies, waits for them, and re-layouts, one_round(): cross_term = turned[col_left, col_right]  47.1 us
    gather x32, local copies, waits for them, and re-layouts, one_round(): diag_left = turned[col_left, col_left]  47.1 us
    gather x32, local copies, waits for them, and re-layouts, one_round(): col_right = order_row[right_slot]  40.5 us
    gather x32, local copies, waits for them, and re-layouts, one_round(): col_left = order_row[left_slot]  40.5 us
  transfers between devices with their start and end apart: 4, of which 4 were waited for; matrix products, arithmetic and copies ran while one was open for 0% of the time, Pallas kernels for 0%

commit v1 on v0

v1 whole, which is shorter than its diff:
```python
import jax
import jax.numpy as jnp
from jax import lax
from jax.experimental import pallas as pl
from jax.experimental.pallas import tpu as pltpu
from jax.sharding import Mesh, PartitionSpec as P

ROUNDS = 16
EPS = 1e-06
HIGHEST = lax.Precision.HIGHEST
NN = (((1,), (0,)), ((), ()))
NT = (((1,), (1,)), ((), ()))
TN = (((0,), (0,)), ((), ()))
PAIRS = ((0, 0), (0, 1), (1, 1), (2, 2), (2, 3), (3, 3), (0, 2), (0, 3), (1, 2), (1, 3))


def dot(a, b, dims=NN):
    return lax.dot_general(a, b, dims, precision=HIGHEST, preferred_element_type=jnp.float32)


def slot_at(place, turn):
    side, inner = place // 128, place % 128
    k = 16 * (inner % 8) + inner // 8
    moved = jnp.where(side == 0, turn + k, turn + 255 - k)
    moved = jnp.where(moved >= 255, moved - 255, moved)
    return jnp.where((side == 0) & (k == 0), 255, moved)


def place_by_column(order_row, turn, transposed):
    rows = lax.broadcasted_iota(jnp.int32, (256, 256), 0)
    cols = lax.broadcasted_iota(jnp.int32, (256, 256), 1)
    column_slot = (rows == order_row).astype(jnp.float32)
    place_slot = (slot_at(rows, turn) == cols).astype(jnp.float32)
    pair = (column_slot, place_slot) if transposed else (place_slot, column_slot)
    return lax.dot_general(*pair, NT, preferred_element_type=jnp.float32)


def rotation(cross, low, high):
    x = high - low
    y = cross + cross
    ax, ay = jnp.abs(x), jnp.abs(y)
    m = jnp.maximum(ax, ay)
    rm = 1.0 / jnp.maximum(m, 1e-37)
    xs = jnp.where(m > 0.0, ax * rm, 1.0)
    ys = y * rm
    r = lax.rsqrt(xs * xs + ys * ys)
    u = 0.5 + 0.5 * (xs * r)
    ru = lax.rsqrt(u)
    big = u * ru
    small = (0.5 * (ys * r)) * ru
    gap = cross * (small * ru)
    back = x < 0.0
    cs = jnp.where(back, jnp.abs(small), big)
    sn = jnp.where(back, jnp.where(y < 0.0, -big, big), small)
    return cs, sn, jnp.minimum(low, high) - gap, jnp.maximum(low, high) + gap


def one_round(src, dst, dsrc, ddst, cbuf, sbuf):
    row8 = lax.broadcasted_iota(jnp.int32, (8, 128), 0)
    first, last = row8 == 0, row8 == 7

    def put(buf, lead, new):
        top, bottom = new
        for t in range(15):
            tile = top[t + 1] if t else jnp.where(first, top[0], top[1])
            buf[(*lead[0], pl.ds(8 * t, 8))] = tile
            buf[(*lead[1], pl.ds(8 * t + 8, 8))] = bottom[t]
        buf[(*lead[0], pl.ds(120, 8))] = jnp.where(last, bottom[15], pltpu.roll(top[0], 7, 0))
        buf[(*lead[1], pl.ds(0, 8))] = jnp.where(first, top[1], pltpu.roll(bottom[15], 1, 0))

    for a in range(2):
        top, bottom = [], []
        for t in range(16):
            rows = pl.ds(8 * t, 8)
            part = src[a, 0, 0, rows] * src[a, 1, 2, rows] + src[a, 0, 1, rows] * src[a, 1, 3, rows]
            cross = jnp.broadcast_to(jnp.sum(part, axis=1, keepdims=True), (8, 128))
            cs, sn, low, high = rotation(cross, dsrc[a, 0, rows], dsrc[a, 1, rows])
            cbuf[a, rows] = cs
            sbuf[a, rows] = sn
            top.append(low)
            bottom.append(high)
        put(ddst, ((a, 0), (a, 1)), (top, bottom))
    for a in range(2):
        for lane in range(4):
            top, bottom = [], []
            for t in range(16):
                rows = pl.ds(8 * t, 8)
                cs, sn = cbuf[a, rows], sbuf[a, rows]
                p, q = src[a, 0, lane, rows], src[a, 1, lane, rows]
                top.append(cs * p - sn * q)
                bottom.append(sn * p + cs * q)
            put(dst, ((a, 0, lane), (a, 1, lane)), (top, bottom))


def rotate_kernel(g_ref, order_ref, qt_ref, rms_ref, xa, xb, da, db, cbuf, sbuf):
    total_rows = 262144.0

    def solve(grams, order_row):
        start = place_by_column(order_row, 0, False)
        for a in range(2):
            held = dot(start, grams[a])
            both = start * held
            diag = jnp.broadcast_to(jnp.sum(both, axis=1, keepdims=True), (256, 128))
            for side in range(2):
                rows = slice(128 * side, 128 * side + 128)
                da[a, side] = diag[rows]
                for lane in range(2):
                    cols = slice(128 * lane, 128 * lane + 128)
                    xa[a, side, lane] = start[rows, cols]
                    xa[a, side, lane + 2] = held[rows, cols]

        def two_rounds(_, carry):
            one_round(xa, xb, da, db, cbuf, sbuf)
            one_round(xb, xa, db, da, cbuf, sbuf)
            return carry

        lax.fori_loop(0, ROUNDS // 2, two_rounds, 0)
        end = place_by_column(order_row, ROUNDS, True)
        basis, held, diag = [], [], []
        for a in range(2):
            sides = [
                jnp.concatenate([jnp.concatenate([xa[a, side, lane] for side in range(2)], axis=0) for lane in range(4)], axis=1)
            ][0]
            back = dot(end, sides)
            basis.append(back[:, :256])
            held.append(back[:, 256:])
            place_diag = jnp.concatenate([da[a, 0], da[a, 1]], axis=0)
            diag.append(dot(place_diag[:, :8], end, (((0,), (1,)), ((), ()))))
        return basis, held, diag

    def square(i, j, k):
        b = g_ref[j]
        return jnp.concatenate(
            [jnp.concatenate([g_ref[i], b], axis=1), jnp.concatenate([b.T, g_ref[k]], axis=1)], axis=0
        )

    basis, held, _ = solve([square(0, 1, 2), square(3, 4, 5)], order_ref[0:1, :])
    turned = [dot(basis[a], held[a], NT) for a in range(2)]
    between = jnp.concatenate(
        [jnp.concatenate([g_ref[6], g_ref[7]], axis=1), jnp.concatenate([g_ref[8], g_ref[9]], axis=1)], axis=0
    )
    cross = dot(dot(basis[0], between), basis[1], NT)
    grams = []
    for a in range(2):
        half = slice(128 * a, 128 * a + 128)
        b = cross[half, half]
        grams.append(
            jnp.concatenate(
                [
                    jnp.concatenate([turned[0][half, half], b], axis=1),
                    jnp.concatenate([b.T, turned[1][half, half]], axis=1),
                ],
                axis=0,
            )
        )
    basis1, _, diag = solve(grams, order_ref[1:2, :])
    for a in range(2):
        half = slice(128 * a, 128 * a + 128)
        qt_ref[a, :, :256] = dot(basis1[a][:, :128], basis[0][half, :])
        qt_ref[a, :, 256:] = dot(basis1[a][:, 128:], basis[1][half, :])
        rms = jnp.sqrt(jnp.maximum(diag[a], 0.0) / total_rows + EPS)
        rms_ref[a] = rms[:, :128]
        rms_ref[a + 2] = rms[:, 128:]


def rotate(g, order):
    return pl.pallas_call(
        rotate_kernel,
        out_shape=(
            jax.ShapeDtypeStruct((2, 256, 512), jnp.float32),
            jax.ShapeDtypeStruct((4, 8, 128), jnp.float32),
        ),
        in_specs=[pl.BlockSpec(memory_space=pltpu.VMEM)] * 2,
        out_specs=[pl.BlockSpec(memory_space=pltpu.VMEM)] * 2,
        scratch_shapes=[
            pltpu.VMEM((2, 2, 4, 128, 128), jnp.float32),
            pltpu.VMEM((2, 2, 4, 128, 128), jnp.float32),
            pltpu.VMEM((2, 2, 128, 128), jnp.float32),
            pltpu.VMEM((2, 2, 128, 128), jnp.float32),
            pltpu.VMEM((2, 128, 128), jnp.float32),
            pltpu.VMEM((2, 128, 128), jnp.float32),
        ],
        compiler_params=pltpu.CompilerParams(vmem_limit_bytes=48 * 1024 * 1024),
    )(g, order)


def gram_kernel(m_ref, g_ref):
    joined = [jnp.concatenate([m_ref[2 * a], m_ref[2 * a + 1]], axis=1) for a in range(2)]
    first = dot(joined[0], joined[0], TN)
    second = dot(joined[1], joined[1], TN)
    between = dot(joined[0], joined[1], TN)
    low, high = slice(0, 128), slice(128, 256)
    for i, whole in enumerate((first, second)):
        g_ref[3 * i] = whole[low, low]
        g_ref[3 * i + 1] = whole[low, high]
        g_ref[3 * i + 2] = whole[high, high]
    g_ref[6] = between[low, low]
    g_ref[7] = between[low, high]
    g_ref[8] = between[high, low]
    g_ref[9] = between[high, high]


def density_kernel(m_ref, qt_ref, out_ref):
    joined = jnp.concatenate([m_ref[c] for c in range(4)], axis=1)
    for a in range(2):
        turned = dot(joined, qt_ref[a], NT)
        squares = turned * turned
        out_ref[a] = squares[:, :128]
        out_ref[a + 2] = squares[:, 128:]


def in_vmem(kernel, out_shape, count):
    return pl.pallas_call(
        kernel,
        out_shape=jax.ShapeDtypeStruct(out_shape, jnp.float32),
        in_specs=[pl.BlockSpec(memory_space=pltpu.VMEM)] * count,
        out_specs=pl.BlockSpec(memory_space=pltpu.VMEM),
        compiler_params=pltpu.CompilerParams(vmem_limit_bytes=48 * 1024 * 1024),
    )


def exchange(parts, axis):
    return lax.all_to_all(parts, axis, 0, 0, tiled=True)


def sum_part(value, axis):
    count = lax.axis_size(axis)
    return exchange(value.reshape(count, value.shape[0] // count, 128), axis).sum(0)


def collect(value, axis):
    return exchange(jnp.broadcast_to(value[None], (lax.axis_size(axis), *value.shape)), axis)


def local(matrix, order):
    blocks = exchange(matrix.reshape(4, 512, 128), "x")
    gram = in_vmem(gram_kernel, (10, 128, 128), 1)(blocks).reshape(1280, 128)
    for axis in ("core", "x", "y"):
        gram = sum_part(gram, axis)
    gram = collect(gram, "z").sum(0)
    for axis in ("y", "x", "core"):
        gram = collect(gram, axis).reshape(-1, 128)
    turns, rms = rotate(gram.reshape(10, 128, 128), order)
    density = exchange(in_vmem(density_kernel, (4, 512, 128), 2)(blocks, turns), "x")
    own = lax.dynamic_index_in_dim(rms, lax.axis_index("x"), 0, keepdims=False)
    return density.reshape(2048, 128), own[0]


def solution(mesh):
    fine = Mesh(mesh.devices.reshape(8, 8, 2, 4), ("z", "y", "core", "x"))
    rows = ("z", "y", "core")
    return jax.shard_map(
        local,
        mesh=fine,
        in_specs=(P(rows, "x"), P()),
        out_specs=(P(rows, "x"), P("x")),
        check_vma=False,
    )
```

time: 1050 us -> 136 us (0.13)
  waiting for transfers between devices: 428 us -> 14.3 us
  local copies, waits for them, and re-layouts: 224 us -> 1.6 us
  blocking collectives: 248 us -> 94.4 us
  matrix products: 107 us -> 0 us
  Pallas kernels: 0 us -> 20.7 us
  other arithmetic: 17.6 us -> 0.08 us
  between operations: 14.2 us -> 0.73 us
    psum x2 -> x0, waiting for transfers between devices: 387 us -> none  [local(): gram_total = lax.psum(partial_value, 'rows')]
    psum x1 -> x0, blocking collectives: 248 us -> none  [local(): squares_sum = lax.psum(jnp.sum(density, axis=0), 'rows')]
    gather x160 -> x0, local copies, waits for them, and re-layouts: 222 us -> none  [the longest x32 47.1 us: one_round(): diag_right = turned[col_right, col_right]]
    dot_general x132 -> x0, matrix products: 107 us -> none  [exact_dot(): jnp.dot(left, right, precision=lax.Precision.HIGHEST, preferred_element_t...]
    all_to_all x0 -> x8, blocking collectives: none -> 94.4 us  [exchange(): return lax.all_to_all(parts, axis, 0, 0, tiled=True)]
    ppermute x2 -> x0, waiting for transfers between devices: 40.1 us -> none  [partner_2(): return lax.ppermute(block, axis, route)]
    pallas_call x0 -> x3, Pallas kernels: none -> 20.7 us  [the longest x1 16.3 us: rotate(): pl.pallas_call(rotate_kernel, out_shape=(jax.ShapeDtypeStruct((2, 256, 51...]
    all_to_all x0 -> x1, waiting for transfers between devices: none -> 14.3 us  [exchange(): return lax.all_to_all(parts, axis, 0, 0, tiled=True)]
  transfers between devices with their start and end apart: 4 -> 1, of which waited for: 4 -> 1; matrix products, arithmetic and copies ran while one was open for 0% -> 0% of each run, Pallas kernels for 0% -> 0%
where the time goes in v1:
time: 136 us; the launch traced here: 135 us
  blocking collectives  94.4 us (69%)
  Pallas kernels  20.7 us (15%)
  waiting for transfers between devices  14.3 us (11%)
  starting transfers between devices  3.52 us (3%)
  local copies, waits for them, and re-layouts  1.6 us (1%)
    all_to_all x8, blocking collectives, exchange(): return lax.all_to_all(parts, axis, 0, 0, tiled=True)  94.4 us
    pallas_call x1, Pallas kernels, rotate(): pl.pallas_call(rotate_kernel, out_shape=(jax.ShapeDtypeStruct((2, 256, 51...  16.3 us
    all_to_all x1, waiting for transfers between devices, exchange(): return lax.all_to_all(parts, axis, 0, 0, tiled=True)  14.3 us
    all_to_all x1, starting transfers between devices, exchange(): return lax.all_to_all(parts, axis, 0, 0, tiled=True)  3.52 us
    pallas_call x1, Pallas kernels, local(): in_vmem(density_kernel, (4, 512, 128), 2)(blocks, turns)  2.83 us
  transfers between devices with their start and end apart: 1, of which 1 were waited for; matrix products, arithmetic and copies ran while one was open for 0% of the time, Pallas kernels for 0%

profile of v1, /device:TPU:1, one launch (start us, length us, event | category | flops | bytes accessed | tf_op | source)
XLA Modules:
  0.0 135.3 jit_solution(11937849678036862570)
XLA Ops:
  0.6 14.6 %all_to_all.45.m_ref = f32[4,512,128]{2,1,0:T(8,128)S(1)} all-to-all(f32[4,512,128]{2,1,0:T(8,128)} %bitcast.13), channel_id=1, replica_groups=mesh['z'=8,'y'=8,'core'=2,'x'=4] {'x'}, dimensions={0} | all-to-all | bytes 2097152 | tf_op jit(solution)/shard_map/all_to_all | solution.py:223
  15.2 1.5 %shard_map.41 = f32[10,128,128]{2,1,0:T(8,128)S(1)} custom-call(f32[4,512,128]{2,1,0:T(8,128)S(1)} %all_to_all.45.m_ref), custom_call_target="tpu_custom_call" | custom-call | tf_op jit(solution)/shard_map/pallas_call | solution.py:237
  16.8 10.6 %all_to_all.46 = f32[2,640,128]{2,1,0:T(8,128)S(1)} all-to-all(f32[2,640,128]{2,1,0:T(8,128)S(1)} %bitcast.9), channel_id=1, replica_groups=mesh['z'=8,'y'=8,'core'=2,'x'=4] {'core'}, dimensions={0} | all-to-all | bytes 1310720 | tf_op jit(solution)/shard_map/all_to_all | solution.py:223
  27.4 9.2 %all_to_all.47 = f32[4,160,128]{2,1,0:T(8,128)S(1)} all-to-all(f32[4,160,128]{2,1,0:T(8,128)S(1)} %bitcast.11), channel_id=1, replica_groups=mesh['z'=8,'y'=8,'core'=2,'x'=4] {'x'}, dimensions={0} | all-to-all | bytes 655360 | tf_op jit(solution)/shard_map/all_to_all | solution.py:223
  36.6 13.9 %all_to_all.48 = f32[8,20,128]{2,1,0:T(8,128)S(1)} all-to-all(f32[8,20,128]{2,1,0:T(8,128)S(1)} %reshape.24), channel_id=1, replica_groups=mesh['z'=8,'y'=8,'core'=2,'x'=4] {'y'}, dimensions={0} | all-to-all | bytes 163840 | tf_op jit(solution)/shard_map/all_to_all | solution.py:223
  50.5 17.5 %all_to_all.49 = f32[8,20,128]{2,1,0:T(8,128)S(1)} all-to-all(f32[8,20,128]{2,1,0:T(8,128)S(1)} %broadcast_in_dim.12), channel_id=1, replica_groups=mesh['z'=8,'y'=8,'core'=2,'x'=4] {'z'}, dimensions={0} | all-to-all | bytes 163840 | tf_op jit(solution)/shard_map/all_to_all | solution.py:223
  68.1 10.0 %all_to_all.50 = f32[8,20,128]{2,1,0:T(8,128)S(1)} all-to-all(f32[8,20,128]{2,1,0:T(8,128)S(1)} %broadcast_in_dim.13), channel_id=1, replica_groups=mesh['z'=8,'y'=8,'core'=2,'x'=4] {'y'}, dimensions={0} | all-to-all | bytes 163840 | tf_op jit(solution)/shard_map/all_to_all | solution.py:223
  78.1 8.3 %all_to_all.51 = f32[4,160,128]{2,1,0:T(8,128)S(1)} all-to-all(f32[4,160,128]{2,1,0:T(8,128)S(1)} %broadcast_in_dim.29), channel_id=1, replica_groups=mesh['z'=8,'y'=8,'core'=2,'x'=4] {'x'}, dimensions={0} | all-to-all | bytes 655360 | tf_op jit(solution)/shard_map/all_to_all | solution.py:223
  86.4 0.0 copy-start
  86.4 10.4 %all_to_all.52 = f32[2,640,128]{2,1,0:T(8,128)S(1)} all-to-all(f32[2,640,128]{2,1,0:T(8,128)S(1)} %broadcast_in_dim.31), channel_id=1, replica_groups=mesh['z'=8,'y'=8,'core'=2,'x'=4] {'core'}, dimensions={0} | all-to-all | bytes 1310720 | tf_op jit(solution)/shard_map/all_to_all | solution.py:223
  96.8 0.0 copy-done
  96.8 16.3 %shard_map.42 = (f32[2,256,512]{2,1,0:T(8,128)S(1)}, f32[4,8,128]{2,1,0:T(8,128)S(1)}) custom-call(f32[10,128,128]{2,1,0:T(8,128)S(1)} %bitcast.8, s32[2,256]{1,0:T(2,128)S(1)} %copy-done), custom_call_target="tpu_custom_call" | custom-call | tf_op jit(solution)/shard_map/pallas_call | solution.py:167
  113.1 2.8 %shard_map.43 = f32[4,512,128]{2,1,0:T(8,128)} custom-call(f32[4,512,128]{2,1,0:T(8,128)S(1)} %all_to_all.45.m_ref, f32[2,256,512]{2,1,0:T(8,128)S(1)} %get-tuple-element.4.qt_ref), custom_call_target="tpu_custom_call" | custom-call | tf_op jit(solution)/shard_map/pallas_call | solution.py:244
  115.9 3.5 %all-to-all-start.8 = ((f32[4,512,128]{2,1,0:T(8,128)}), f32[4,512,128]{2,1,0:T(8,128)S(1)}, u32[]{:S(2)}, u32[]{:S(2)}) async-start(f32[4,512,128]{2,1,0:T(8,128)} %shard_map.43), calls=%async_computation.8 | async-start | bytes 2097152 | tf_op jit(solution)/shard_map/all_to_all | solution.py:223
  119.5 0.5 slice_bitcast_fusion
  120.0 14.3 %all-to-all-done.8 = f32[4,512,128]{2,1,0:T(8,128)S(1)} async-done(((f32[4,512,128]{2,1,0:T(8,128)}), f32[4,512,128]{2,1,0:T(8,128)S(1)}, u32[]{:S(2)}, u32[]{:S(2)}) %all-to-all-start.8) | async-done | bytes 1048608 | tf_op jit(solution)/shard_map/all_to_all | solution.py:223
  134.3 1.0 copy.7
  (11 shorter events, 0.2 us)
Async XLA Ops:
  86.4 10.4 %copy-start = (s32[2,256]{1,0:T(2,128)S(1)}, s32[2,256]{1,0:T(2,128)}, u32[]{:S(2)}) copy-start(s32[2,256]{1,0:T(2,128)} %order_ref.1) | copy-start | bytes 6148
  115.9 18.3 %all-to-all-start.8 = ((f32[4,512,128]{2,1,0:T(8,128)}), f32[4,512,128]{2,1,0:T(8,128)S(1)}, u32[]{:S(2)}, u32[]{:S(2)}) async-start(f32[4,512,128]{2,1,0:T(8,128)} %shard_map.43), calls=%async_computation.8 | async-start | bytes 2097152 | tf_op jit(solution)/shard_map/all_to_all | solution.py:223

commit v2 on v1

v2 whole, which is shorter than its diff:
```python
import jax
import jax.numpy as jnp
from jax import lax
from jax.experimental import pallas as pl
from jax.experimental.pallas import tpu as pltpu
from jax.sharding import Mesh, PartitionSpec as P

ROUNDS = 16
ROWS = 262144
EPS = 1e-06
HIGHEST = lax.Precision.HIGHEST
NN = (((1,), (0,)), ((), ()))
NT = (((1,), (1,)), ((), ()))
TN = (((0,), (0,)), ((), ()))
PAIRS = ((0, 0), (0, 1), (1, 1), (2, 2), (2, 3), (3, 3), (0, 2), (0, 3), (1, 2), (1, 3))
LIMIT = pltpu.CompilerParams(vmem_limit_bytes=48 * 1024 * 1024)
VMEM = pl.BlockSpec(memory_space=pltpu.VMEM)


def dot(a, b, dims=NN):
    return lax.dot_general(a, b, dims, precision=HIGHEST, preferred_element_type=jnp.float32)


def short_dot(a, b, dims=NN):
    return lax.dot_general(a, b, dims, preferred_element_type=jnp.float32)


def split(value, count):
    parts = []
    for _ in range(count):
        part = value.astype(jnp.bfloat16)
        value = value - part.astype(jnp.float32)
        parts.append(part)
    return parts


def pick(onehot, value, dims=NN):
    high, mid, low = (short_dot(onehot, part, dims) for part in split(value, 3))
    return high + (mid + low)


def slot_at(place, turn):
    side, inner = place // 128, place % 128
    k = 16 * (inner % 8) + inner // 8
    moved = jnp.where(side == 0, turn + k, turn + 255 - k)
    moved = jnp.where(moved >= 255, moved - 255, moved)
    return jnp.where((side == 0) & (k == 0), 255, moved)


def places_kernel(order_ref, start_ref, end_ref):
    rows = lax.broadcasted_iota(jnp.int32, (256, 256), 0)
    cols = lax.broadcasted_iota(jnp.int32, (256, 256), 1)
    first = (slot_at(rows, 0) == cols).astype(jnp.bfloat16)
    last = (slot_at(rows, ROUNDS) == cols).astype(jnp.bfloat16)
    for step in range(2):
        column_slot = (rows == order_ref[step : step + 1, :]).astype(jnp.bfloat16)
        start_ref[step] = short_dot(first, column_slot, NT).astype(jnp.bfloat16)
        end_ref[step] = short_dot(column_slot, last, NT).astype(jnp.bfloat16)


def rotation(cross, low, high):
    x = high - low
    y = cross + cross
    ax = jnp.abs(x)
    yy = y * y
    hh = x * x + yy + 1e-37
    h = hh * lax.rsqrt(hh)
    w = h + ax
    n = lax.rsqrt(w * w + yy)
    big = w * n
    small = y * n
    gap = h * small * small
    back = x < 0.0
    cs = jnp.where(back, small, big)
    sn = jnp.where(back, big, small)
    return cs, sn, jnp.minimum(low, high) - gap, jnp.maximum(low, high) + gap


def one_round(count, src, dst, dsrc, ddst, cbuf, sbuf):
    row8 = lax.broadcasted_iota(jnp.int32, (8, 128), 0)
    first, last = row8 == 0, row8 == 7

    def put(buf, lead, new):
        top, bottom = new
        for t in range(15):
            tile = top[t + 1] if t else jnp.where(first, top[0], top[1])
            buf[(*lead[0], pl.ds(8 * t, 8))] = tile
            buf[(*lead[1], pl.ds(8 * t + 8, 8))] = bottom[t]
        buf[(*lead[0], pl.ds(120, 8))] = jnp.where(last, bottom[15], pltpu.roll(top[0], 7, 0))
        buf[(*lead[1], pl.ds(0, 8))] = jnp.where(first, top[1], pltpu.roll(bottom[15], 1, 0))

    for a in range(count):
        top, bottom = [], []
        for t in range(16):
            rows = pl.ds(8 * t, 8)
            part = src[a, 0, 0, rows] * src[a, 1, 2, rows] + src[a, 0, 1, rows] * src[a, 1, 3, rows]
            cross = jnp.broadcast_to(jnp.sum(part, axis=1, keepdims=True), (8, 128))
            cs, sn, low, high = rotation(cross, dsrc[a, 0, rows], dsrc[a, 1, rows])
            cbuf[a, rows] = cs
            sbuf[a, rows] = sn
            top.append(low)
            bottom.append(high)
        put(ddst, ((a, 0), (a, 1)), (top, bottom))
    for a in range(count):
        for lane in range(4):
            top, bottom = [], []
            for t in range(16):
                rows = pl.ds(8 * t, 8)
                cs, sn = cbuf[a, rows], sbuf[a, rows]
                p, q = src[a, 0, lane, rows], src[a, 1, lane, rows]
                top.append(cs * p - sn * q)
                bottom.append(sn * p + cs * q)
            put(dst, ((a, 0, lane), (a, 1, lane)), (top, bottom))


def rotate_kernel(x_ref, g_ref, start_ref, end_ref, q_ref, rms_ref, xa, xb, da, db, cbuf, sbuf):
    own_pair, own_side = x_ref[0] % 2, x_ref[0] // 2
    half = pl.ds(pl.multiple_of(128 * own_pair, 128), 128)

    def solve(grams, step):
        start = start_ref[step]
        start32 = start.astype(jnp.float32)
        for a, gram in enumerate(grams):
            held = pick(start, gram)
            diag = jnp.broadcast_to(jnp.sum(start32 * held, axis=1, keepdims=True), (256, 128))
            for side in range(2):
                rows = slice(128 * side, 128 * side + 128)
                da[a, side] = diag[rows]
                for lane in range(2):
                    cols = slice(128 * lane, 128 * lane + 128)
                    xa[a, side, lane] = start32[rows, cols]
                    xa[a, side, lane + 2] = held[rows, cols]

        def two_rounds(_, carry):
            one_round(len(grams), xa, xb, da, db, cbuf, sbuf)
            one_round(len(grams), xb, xa, db, da, cbuf, sbuf)
            return carry

        lax.fori_loop(0, ROUNDS // 2, two_rounds, 0)

    def placed(a, lanes):
        sides = [jnp.concatenate([xa[a, side, lane] for lane in lanes], axis=1) for side in range(2)]
        return jnp.concatenate(sides, axis=0)

    def square(a, b, d):
        return jnp.concatenate([jnp.concatenate([a, b], axis=1), jnp.concatenate([b.T, d], axis=1)], axis=0)

    solve([square(g_ref[i], g_ref[i + 1], g_ref[i + 2]) for i in (0, 3)], 0)
    end = end_ref[0, half, :]
    both = [pick(end, placed(a, range(4))) for a in range(2)]
    basis = [value[:, :256] for value in both]
    turned = [dot(value[:, :256], value[:, 256:], NT) for value in both]
    between = jnp.concatenate(
        [jnp.concatenate([g_ref[6], g_ref[7]], axis=1), jnp.concatenate([g_ref[8], g_ref[9]], axis=1)], axis=0
    )
    cross = dot(dot(basis[0], between), basis[1], NT)
    solve([square(turned[0], cross, turned[1])], 1)
    end = end_ref[1, pl.ds(pl.multiple_of(128 * own_side, 128), 128), :]
    last = pick(end, placed(0, range(2)))
    turns = jnp.concatenate([dot(last[:, :128], basis[0]), dot(last[:, 128:], basis[1])], axis=1)
    high, low = split(turns, 2)
    q_ref[:128] = high
    q_ref[128:] = low
    diag = jnp.concatenate([da[0, 0], da[0, 1]], axis=0)
    squares = sum(short_dot(part[:, :8], end, (((0,), (1,)), ((), ()))) for part in reversed(split(diag, 3)))
    rms_ref[...] = jnp.sqrt(jnp.maximum(squares, 0.0) / ROWS + EPS)


def rotate(x_index, gram, start, end):
    return pl.pallas_call(
        rotate_kernel,
        out_shape=(
            jax.ShapeDtypeStruct((256, 512), jnp.bfloat16),
            jax.ShapeDtypeStruct((8, 128), jnp.float32),
        ),
        in_specs=[pl.BlockSpec(memory_space=pltpu.SMEM), VMEM, VMEM, VMEM],
        out_specs=[VMEM, VMEM],
        scratch_shapes=[
            pltpu.VMEM((2, 2, 4, 128, 128), jnp.float32),
            pltpu.VMEM((2, 2, 4, 128, 128), jnp.float32),
            pltpu.VMEM((2, 2, 128, 128), jnp.float32),
            pltpu.VMEM((2, 2, 128, 128), jnp.float32),
            pltpu.VMEM((2, 128, 128), jnp.float32),
            pltpu.VMEM((2, 128, 128), jnp.float32),
        ],
        compiler_params=LIMIT,
    )(x_index, gram, start, end)


def places(order):
    return pl.pallas_call(
        places_kernel,
        out_shape=(jax.ShapeDtypeStruct((2, 256, 256), jnp.bfloat16),) * 2,
        in_specs=[VMEM],
        out_specs=[VMEM, VMEM],
        compiler_params=LIMIT,
    )(order)


def gram_kernel(m_ref, g_ref):
    joined = [jnp.concatenate([m_ref[2 * a], m_ref[2 * a + 1]], axis=1) for a in range(2)]
    low, high = slice(0, 128), slice(128, 256)
    for i in range(2):
        whole = dot(joined[i], joined[i], TN)
        g_ref[3 * i] = whole[low, low]
        g_ref[3 * i + 1] = whole[low, high]
        g_ref[3 * i + 2] = whole[high, high]
    between = dot(joined[0], joined[1], TN)
    g_ref[6] = between[low, low]
    g_ref[7] = between[low, high]
    g_ref[8] = between[high, low]
    g_ref[9] = between[high, high]


def grams(blocks):
    return pl.pallas_call(
        gram_kernel,
        out_shape=jax.ShapeDtypeStruct((10, 128, 128), jnp.float32),
        in_specs=[VMEM],
        out_specs=VMEM,
        compiler_params=LIMIT,
    )(blocks)


def density_kernel(m_ref, q_ref, out_ref):
    joined = jnp.concatenate([m_ref[c] for c in range(4)], axis=1)
    high, low = split(joined, 2)
    wide = short_dot(high, q_ref[...], NT)
    turned = wide[:, :128] + (wide[:, 128:] + short_dot(low, q_ref[:128, :], NT))
    out_ref[...] = turned * turned


def densities(whole, turns):
    rows = whole.shape[1]
    return pl.pallas_call(
        density_kernel,
        grid=(4,),
        out_shape=jax.ShapeDtypeStruct((rows, 128), jnp.float32),
        in_specs=[
            pl.BlockSpec((4, rows // 4, 128), lambda i: (0, i, 0)),
            pl.BlockSpec((256, 512), lambda i: (0, 0)),
        ],
        out_specs=pl.BlockSpec((rows // 4, 128), lambda i: (i, 0)),
        compiler_params=LIMIT,
    )(whole, turns)


def exchange(parts, axis):
    return lax.all_to_all(parts, axis, 0, 0, tiled=True)


def sum_part(value, axis):
    count = lax.axis_size(axis)
    return exchange(value.reshape(count, value.shape[0] // count, 128), axis).sum(0)


def collect(value, axis):
    return exchange(jnp.broadcast_to(value[None], (lax.axis_size(axis), *value.shape)), axis)


def local(matrix, order):
    start, end = places(order)
    blocks = exchange(matrix.reshape(4, 512, 128), "x")
    matrix, blocks = lax.optimization_barrier((matrix, blocks))
    whole = lax.all_gather(matrix, "x")
    gram = grams(blocks).reshape(1280, 128)
    for axis in ("core", "x", "y"):
        gram = sum_part(gram, axis)
    gram = collect(gram, "z").sum(0)
    for axis in ("y", "x", "core"):
        gram = collect(gram, axis).reshape(-1, 128)
    x_index = lax.axis_index("x").astype(jnp.int32).reshape(1)
    turns, rms = rotate(x_index, gram.reshape(10, 128, 128), start, end)
    return densities(whole, turns), rms[0]


def solution(mesh):
    fine = Mesh(mesh.devices.reshape(8, 8, 2, 4), ("z", "y", "core", "x"))
    rows = ("z", "y", "core")
    return jax.shard_map(
        local,
        mesh=fine,
        in_specs=(P(rows, "x"), P()),
        out_specs=(P(rows, "x"), P("x")),
        check_vma=False,
    )
```

time: 136 us -> 128 us (0.941)
  between operations: 0.73 us -> 14.1 us
  waiting for transfers between devices: 14.3 us -> 5.45 us
  blocking collectives: 94.4 us -> 86.1 us
  Pallas kernels: 20.7 us -> 14.9 us
  local copies, waits for them, and re-layouts: 1.6 us -> 3.54 us
    all_to_all x1, waiting for transfers between devices: 14.3 us -> 5.43 us  [exchange(): return lax.all_to_all(parts, axis, 0, 0, tiled=True)]
    all_to_all x8 -> x7, blocking collectives: 94.4 us -> 86.1 us  [exchange(): return lax.all_to_all(parts, axis, 0, 0, tiled=True)]
    pallas_call x3 -> x4, Pallas kernels: 20.7 us -> 14.9 us  [the longest x1 9.88 us: rotate(): pl.pallas_call(rotate_kernel, out_shape=(jax.ShapeDtypeStruct((256, 512),...]
  transfers between devices with their start and end apart: 1 -> 2, of which waited for: 1 -> 1; matrix products, arithmetic and copies ran while one was open for 0% -> 1% of each run, Pallas kernels for 0% -> 9%
where the time goes in v2:
time: 128 us
  blocking collectives  86.1 us (67%)
  Pallas kernels  14.9 us (12%)
  between operations  14.1 us (11%)
  waiting for transfers between devices  5.45 us (4%)
  local copies, waits for them, and re-layouts  3.54 us (3%)
  starting transfers between devices  3.49 us (3%)
    all_to_all x7, blocking collectives, exchange(): return lax.all_to_all(parts, axis, 0, 0, tiled=True)  86.1 us
    pallas_call x1, Pallas kernels, rotate(): pl.pallas_call(rotate_kernel, out_shape=(jax.ShapeDtypeStruct((256, 512),...  9.88 us
    all_to_all x1, waiting for transfers between devices, exchange(): return lax.all_to_all(parts, axis, 0, 0, tiled=True)  5.43 us
    all_to_all x1, starting transfers between devices, exchange(): return lax.all_to_all(parts, axis, 0, 0, tiled=True)  3.45 us
    pallas_call x1, Pallas kernels, densities(): pl.pallas_call(density_kernel, grid=(4,), out_shape=jax.ShapeDtypeStruct(...  3.04 us
  transfers between devices with their start and end apart: 2, of which 1 were waited for; matrix products, arithmetic and copies ran while one was open for 1% of the time, Pallas kernels for 9%

profile of v2, /device:TPU:1, one launch (start us, length us, event | category | flops | bytes accessed | tf_op | source)
XLA Modules:
  0.0 127.6 jit_solution(16949499225834244284)
XLA Ops:
  7.2 0.0 all-gather.3.cloned.1.call-start
  7.2 14.6 %all_to_all.40.m_ref = f32[4,512,128]{2,1,0:T(8,128)S(1)} all-to-all(f32[4,512,128]{2,1,0:T(8,128)} %bitcast.12), channel_id=1, replica_groups=mesh['z'=8,'y'=8,'core'=2,'x'=4] {'x'}, dimensions={0} | all-to-all | bytes 2097152 | tf_op jit(solution)/shard_map/all_to_all | solution.py:249
  21.8 0.0 copy-start.1
  21.8 0.0 all-gather.3.cloned.1.call-update
  21.8 1.5 %shard_map.41 = f32[10,128,128]{2,1,0:T(8,128)S(1)} custom-call(f32[4,512,128]{2,1,0:T(8,128)S(1)} %all_to_all.40.m_ref), custom_call_target="tpu_custom_call" | custom-call | tf_op jit(solution)/shard_map/pallas_call | solution.py:216
  23.4 10.6 %all_to_all.41 = f32[2,640,128]{2,1,0:T(8,128)S(1)} all-to-all(f32[2,640,128]{2,1,0:T(8,128)S(1)} %bitcast.11), channel_id=1, replica_groups=mesh['z'=8,'y'=8,'core'=2,'x'=4] {'core'}, dimensions={0} | all-to-all | bytes 1310720 | tf_op jit(solution)/shard_map/all_to_all | solution.py:249
  34.0 9.2 %all_to_all.42 = f32[4,160,128]{2,1,0:T(8,128)S(1)} all-to-all(f32[4,160,128]{2,1,0:T(8,128)S(1)} %bitcast.13), channel_id=1, replica_groups=mesh['z'=8,'y'=8,'core'=2,'x'=4] {'x'}, dimensions={0} | all-to-all | bytes 655360 | tf_op jit(solution)/shard_map/all_to_all | solution.py:249
  43.2 13.9 %all_to_all.43 = f32[8,20,128]{2,1,0:T(8,128)S(1)} all-to-all(f32[8,20,128]{2,1,0:T(8,128)S(1)} %reshape.23), channel_id=1, replica_groups=mesh['z'=8,'y'=8,'core'=2,'x'=4] {'y'}, dimensions={0} | all-to-all | bytes 163840 | tf_op jit(solution)/shard_map/all_to_all | solution.py:249
  57.1 17.5 %all_to_all.44 = f32[8,20,128]{2,1,0:T(8,128)S(1)} all-to-all(f32[8,20,128]{2,1,0:T(8,128)S(1)} %broadcast_in_dim.12), channel_id=1, replica_groups=mesh['z'=8,'y'=8,'core'=2,'x'=4] {'z'}, dimensions={0} | all-to-all | bytes 163840 | tf_op jit(solution)/shard_map/all_to_all | solution.py:249
  74.7 10.0 %all_to_all.45 = f32[8,20,128]{2,1,0:T(8,128)S(1)} all-to-all(f32[8,20,128]{2,1,0:T(8,128)S(1)} %broadcast_in_dim.13), channel_id=1, replica_groups=mesh['z'=8,'y'=8,'core'=2,'x'=4] {'y'}, dimensions={0} | all-to-all | bytes 163840 | tf_op jit(solution)/shard_map/all_to_all | solution.py:249
  84.6 0.7 broadcast_in_dim.29
  85.4 3.5 %all-to-all-start.6 = ((f32[4,160,128]{2,1,0:T(8,128)}), f32[4,160,128]{2,1,0:T(8,128)S(1)}, u32[]{:S(2)}, u32[]{:S(2)}) async-start(f32[4,160,128]{2,1,0:T(8,128)} %broadcast_in_dim.29), calls=%async_computation.6 | async-start | bytes 655360 | tf_op jit(solution)/shard_map/all_to_all | solution.py:249
  88.9 0.0 copy-done.1
  88.9 0.4 shard_map.42
  89.3 5.4 %all-to-all-done.6 = f32[4,160,128]{2,1,0:T(8,128)S(1)} async-done(((f32[4,160,128]{2,1,0:T(8,128)}), f32[4,160,128]{2,1,0:T(8,128)S(1)}, u32[]{:S(2)}, u32[]{:S(2)}) %all-to-all-start.6) | async-done | bytes 327712 | tf_op jit(solution)/shard_map/all_to_all | solution.py:249
  94.7 10.4 %all_to_all.46 = f32[2,640,128]{2,1,0:T(8,128)S(1)} all-to-all(f32[2,640,128]{2,1,0:T(8,128)S(1)} %broadcast_in_dim.31), channel_id=1, replica_groups=mesh['z'=8,'y'=8,'core'=2,'x'=4] {'core'}, dimensions={0} | all-to-all | bytes 1310720 | tf_op jit(solution)/shard_map/all_to_all | solution.py:249
  105.1 9.9 %shard_map.43 = (bf16[256,512]{1,0:T(8,128)(2,1)S(1)}, f32[8,128]{1,0:T(8,128)S(1)}) custom-call(s32[1]{0:T(128)} %bitcast.2.x_ref, f32[10,128,128]{2,1,0:T(8,128)S(1)} %bitcast.10, bf16[2,256,256]{2,1,0:T(8,128)(2,1)S(1)} %get-tuple-element.10.start_ref, bf16[2,256,256]{2,1,0:T(8,128)(2,1)S(1)} %get-tuple-element.11.end_ref), custom_call_target="tpu_custom_call" | custom-call | tf_op jit(solution)/shard_map/pallas_call | solution.py:170
  115.0 0.5 slice_bitcast_fusion
  115.6 0.0 all-gather.3.cloned.1.call-done
  115.6 0.0 copy-start
  115.6 2.2 %copy-done = f32[8192,128]{1,0:T(8,128)S(1)} copy-done((f32[8192,128]{1,0:T(8,128)S(1)}, f32[8192,128]{1,0:T(8,128)}, u32[]{:S(2)}) %copy-start) | copy-done | bytes 4194328
  117.7 3.0 %shard_map.44 = f32[2048,128]{1,0:T(8,128)} custom-call(f32[4,2048,128]{2,1,0:T(8,128)S(1)} %bitcast.9, bf16[256,512]{1,0:T(8,128)(2,1)S(1)} %get-tuple-element.12.q_ref), custom_call_target="tpu_custom_call" | custom-call | tf_op jit(solution)/shard_map/pallas_call | solution.py:235
  (9 shorter events, 0.2 us)
Async XLA Ops:
  7.2 108.4 %all-gather.3.cloned.1.call-start = ((), (), s32[]{:S(2)}) async-start(), calls=%async_computation.8 | async-start | bytes 5242880 | tf_op jit(solution)/shard_map/all_gather | solution.py:265
  21.8 67.1 %copy-start.1 = (s32[2,256]{1,0:T(2,128)S(1)}, s32[2,256]{1,0:T(2,128)}, u32[]{:S(2)}) copy-start(s32[2,256]{1,0:T(2,128)} %order_ref.1) | copy-start | bytes 6148
  85.4 9.3 %all-to-all-start.6 = ((f32[4,160,128]{2,1,0:T(8,128)}), f32[4,160,128]{2,1,0:T(8,128)S(1)}, u32[]{:S(2)}, u32[]{:S(2)}) async-start(f32[4,160,128]{2,1,0:T(8,128)} %broadcast_in_dim.29), calls=%async_computation.6 | async-start | bytes 655360 | tf_op jit(solution)/shard_map/all_to_all | solution.py:249
  115.6 2.2 %copy-start = (f32[8192,128]{1,0:T(8,128)S(1)}, f32[8192,128]{1,0:T(8,128)}, u32[]{:S(2)}) copy-start(f32[8192,128]{1,0:T(8,128)} %all-gather.3.cloned.1.call-done) | copy-start | bytes 12582916
Sparse Core Ops, SparseCore 0:
  22.0 62.0 all-gather.2

commit v3 on v2

--- a/solution.py
+++ b/solution.py
@@ -15,6 +15,9 @@
 PAIRS = ((0, 0), (0, 1), (1, 1), (2, 2), (2, 3), (3, 3), (0, 2), (0, 3), (1, 2), (1, 3))
 LIMIT = pltpu.CompilerParams(vmem_limit_bytes=48 * 1024 * 1024)
 VMEM = pl.BlockSpec(memory_space=pltpu.VMEM)
+SMEM = pl.BlockSpec(memory_space=pltpu.SMEM)
+HBM = pl.BlockSpec(memory_space=pltpu.HBM)
+CHUNKS = 4
 
 
 def dot(a, b, dims=NN):
@@ -113,8 +116,20 @@
             put(dst, ((a, 0, lane), (a, 1, lane)), (top, bottom))
 
 
-def rotate_kernel(x_ref, g_ref, start_ref, end_ref, q_ref, rms_ref, xa, xb, da, db, cbuf, sbuf):
-    own_pair, own_side = x_ref[0] % 2, x_ref[0] // 2
+def rotate_kernel(
+    place_ref, own_ref, other_ref, start_ref, end_ref, whole_ref, out_ref, rms_ref,
+    g_ref, xa, xb, da, db, cbuf, sbuf, held_rows, squares, in_sems, out_sems,
+):
+    rows_each = held_rows.shape[2]
+    fetch = []
+    for i in range(CHUNKS):
+        rows = pl.ds(i * rows_each, rows_each)
+        fetch.append(pltpu.make_async_copy(whole_ref.at[:, rows, :], held_rows.at[i], in_sems.at[i]))
+        fetch[-1].start()
+    core = place_ref[1]
+    g_ref[pl.ds(5 * core, 5)] = own_ref[...]
+    g_ref[pl.ds(5 * (1 - core), 5)] = other_ref[...]
+    own_pair, own_side = place_ref[0] % 2, place_ref[0] // 2
     half = pl.ds(pl.multiple_of(128 * own_pair, 128), 128)
 
     def solve(grams, step):
@@ -158,33 +173,50 @@
     end = end_ref[1, pl.ds(pl.multiple_of(128 * own_side, 128), 128), :]
     last = pick(end, placed(0, range(2)))
     turns = jnp.concatenate([dot(last[:, :128], basis[0]), dot(last[:, 128:], basis[1])], axis=1)
-    high, low = split(turns, 2)
-    q_ref[:128] = high
-    q_ref[128:] = low
     diag = jnp.concatenate([da[0, 0], da[0, 1]], axis=0)
-    squares = sum(short_dot(part[:, :8], end, (((0,), (1,)), ((), ()))) for part in reversed(split(diag, 3)))
-    rms_ref[...] = jnp.sqrt(jnp.maximum(squares, 0.0) / ROWS + EPS)
-
-
-def rotate(x_index, gram, start, end):
+    sums = sum(short_dot(part[:, :8], end, (((0,), (1,)), ((), ()))) for part in reversed(split(diag, 3)))
+    rms_ref[...] = jnp.sqrt(jnp.maximum(sums[:1], 0.0) / ROWS + EPS)
+    turn_high, turn_low = split(turns, 2)
+    both = jnp.concatenate([turn_high, turn_low], axis=0)
+    store = []
+    for i in range(CHUNKS):
+        fetch[i].wait()
+        high, low = split(jnp.concatenate([held_rows[i, c] for c in range(4)], axis=1), 2)
+        wide = short_dot(high, both, NT)
+        value = wide[:, :128] + (wide[:, 128:] + short_dot(low, turn_high, NT))
+        rows = pl.ds(i * rows_each, rows_each)
+        squares[rows, :] = value * value
+        store.append(pltpu.make_async_copy(squares.at[rows, :], out_ref.at[rows, :], out_sems.at[i]))
+        store[-1].start()
+    for copy in store:
+        copy.wait()
+
+
+def rotate(place, own, other, start, end, whole):
+    rows = whole.shape[1]
     return pl.pallas_call(
         rotate_kernel,
         out_shape=(
-            jax.ShapeDtypeStruct((256, 512), jnp.bfloat16),
-            jax.ShapeDtypeStruct((8, 128), jnp.float32),
+            jax.ShapeDtypeStruct((rows, 128), jnp.float32),
+            jax.ShapeDtypeStruct((1, 128), jnp.float32),
         ),
-        in_specs=[pl.BlockSpec(memory_space=pltpu.SMEM), VMEM, VMEM, VMEM],
-        out_specs=[VMEM, VMEM],
+        in_specs=[SMEM, VMEM, VMEM, VMEM, VMEM, HBM],
+        out_specs=[HBM, VMEM],
         scratch_shapes=[
+            pltpu.VMEM((10, 128, 128), jnp.float32),
             pltpu.VMEM((2, 2, 4, 128, 128), jnp.float32),
             pltpu.VMEM((2, 2, 4, 128, 128), jnp.float32),
             pltpu.VMEM((2, 2, 128, 128), jnp.float32),
             pltpu.VMEM((2, 2, 128, 128), jnp.float32),
             pltpu.VMEM((2, 128, 128), jnp.float32),
             pltpu.VMEM((2, 128, 128), jnp.float32),
+            pltpu.VMEM((CHUNKS, 4, rows // CHUNKS, 128), jnp.float32),
+            pltpu.VMEM((rows, 128), jnp.float32),
+            pltpu.SemaphoreType.DMA((CHUNKS,)),
+            pltpu.SemaphoreType.DMA((CHUNKS,)),
         ],
-        compiler_params=LIMIT,
-    )(x_index, gram, start, end)
+        compiler_params=pltpu.CompilerParams(vmem_limit_bytes=52 * 1024 * 1024),
+    )(place, own, other, start, end, whole)
 
 
 def places(order):
@@ -197,52 +229,37 @@
     )(order)
 
 
-def gram_kernel(m_ref, g_ref):
-    joined = [jnp.concatenate([m_ref[2 * a], m_ref[2 * a + 1]], axis=1) for a in range(2)]
+def gram_kernel(core_ref, m_ref, mine_ref, theirs_ref):
+    parts = [split(jnp.concatenate([m_ref[2 * a], m_ref[2 * a + 1]], axis=1), 2) for a in range(2)]
+
+    def product(left, right):
+        (lh, ll), (rh, rl) = left, right
+        small = (short_dot(lh, rl, TN) + short_dot(ll, rh, TN)) + short_dot(ll, rl, TN)
+        return short_dot(lh, rh, TN) + small
+
     low, high = slice(0, 128), slice(128, 256)
-    for i in range(2):
-        whole = dot(joined[i], joined[i], TN)
-        g_ref[3 * i] = whole[low, low]
-        g_ref[3 * i + 1] = whole[low, high]
-        g_ref[3 * i + 2] = whole[high, high]
-    between = dot(joined[0], joined[1], TN)
-    g_ref[6] = between[low, low]
-    g_ref[7] = between[low, high]
-    g_ref[8] = between[high, low]
-    g_ref[9] = between[high, high]
-
-
-def grams(blocks):
+    blocks = []
+    for part in parts:
+        whole = product(part, part)
+        blocks += [whole[low, low], whole[low, high], whole[high, high]]
+    between = product(*parts)
+    blocks += [between[low, low], between[low, high], between[high, low], between[high, high]]
+    for core, halves in enumerate(((mine_ref, theirs_ref), (theirs_ref, mine_ref))):
+
+        @pl.when(core_ref[0] == core)
+        def _(halves=halves):
+            for i, block in enumerate(blocks):
+                halves[i // 5][i % 5] = block
+
+
+def grams(core_index, blocks):
     return pl.pallas_call(
         gram_kernel,
-        out_shape=jax.ShapeDtypeStruct((10, 128, 128), jnp.float32),
-        in_specs=[VMEM],
-        out_specs=VMEM,
+        out_shape=(jax.ShapeDtypeStruct((5, 128, 128), jnp.float32),) * 2,
+        in_specs=[SMEM, VMEM],
+        out_specs=[VMEM, VMEM],
         compiler_params=LIMIT,
-    )(blocks)
-
-
-def density_kernel(m_ref, q_ref, out_ref):
-    joined = jnp.concatenate([m_ref[c] for c in range(4)], axis=1)
-    high, low = split(joined, 2)
-    wide = short_dot(high, q_ref[...], NT)
-    turned = wide[:, :128] + (wide[:, 128:] + short_dot(low, q_ref[:128, :], NT))
-    out_ref[...] = turned * turned
-
-
-def densities(whole, turns):
-    rows = whole.shape[1]
-    return pl.pallas_call(
-        density_kernel,
-        grid=(4,),
-        out_shape=jax.ShapeDtypeStruct((rows, 128), jnp.float32),
-        in_specs=[
-            pl.BlockSpec((4, rows // 4, 128), lambda i: (0, i, 0)),
-            pl.BlockSpec((256, 512), lambda i: (0, 0)),
-        ],
-        out_specs=pl.BlockSpec((rows // 4, 128), lambda i: (i, 0)),
-        compiler_params=LIMIT,
-    )(whole, turns)
+    )(core_index, blocks)
 
 
 def exchange(parts, axis):
@@ -258,20 +275,26 @@
     return exchange(jnp.broadcast_to(value[None], (lax.axis_size(axis), *value.shape)), axis)
 
 
+def swap_cores(value):
+    return lax.ppermute(value, "core", ((0, 1), (1, 0)))
+
+
 def local(matrix, order):
+    place = jnp.stack([lax.axis_index("x"), lax.axis_index("core")]).astype(jnp.int32)
     start, end = places(order)
     blocks = exchange(matrix.reshape(4, 512, 128), "x")
     matrix, blocks = lax.optimization_barrier((matrix, blocks))
     whole = lax.all_gather(matrix, "x")
-    gram = grams(blocks).reshape(1280, 128)
-    for axis in ("core", "x", "y"):
+    mine, theirs = grams(place[1:], blocks)
+    gram = (mine + swap_cores(theirs)).reshape(640, 128)
+    for axis in ("x", "y"):
         gram = sum_part(gram, axis)
     gram = collect(gram, "z").sum(0)
-    for axis in ("y", "x", "core"):
+    for axis in ("y", "x"):
         gram = collect(gram, axis).reshape(-1, 128)
-    x_index = lax.axis_index("x").astype(jnp.int32).reshape(1)
-    turns, rms = rotate(x_index, gram.reshape(10, 128, 128), start, end)
-    return densities(whole, turns), rms[0]
+    own = gram.reshape(5, 128, 128)
+    density, rms = rotate(place, own, swap_cores(own), start, end, whole)
+    return density, rms.reshape(128)
 
 
 def solution(mesh):

time: 128 us -> 122 us (0.953)
  starting transfers between devices: 3.49 us -> 17 us
  blocking collectives: 86.1 us -> 73.4 us
  local copies, waits for them, and re-layouts: 3.54 us -> 0.06 us
  waiting for transfers between devices: 5.45 us -> 2 us
    ppermute x0 -> x2, starting transfers between devices: none -> 17 us  [swap_cores(): return lax.ppermute(value, 'core', ((0, 1), (1, 0)))]
    all_to_all x7 -> x6, blocking collectives: 86.1 us -> 73.4 us  [exchange(): return lax.all_to_all(parts, axis, 0, 0, tiled=True)]
    all_to_all x1 -> x0, waiting for transfers between devices: 5.43 us -> none  [exchange(): return lax.all_to_all(parts, axis, 0, 0, tiled=True)]
    all_to_all x1 -> x0, starting transfers between devices: 3.45 us -> none  [exchange(): return lax.all_to_all(parts, axis, 0, 0, tiled=True)]
    unnamed x4 -> x2, local copies, waits for them, and re-layouts: 2.19 us -> 0.01 us
    ppermute x0 -> x2, waiting for transfers between devices: none -> 1.98 us  [swap_cores(): return lax.ppermute(value, 'core', ((0, 1), (1, 0)))]
    pallas_call x3 -> x2, Pallas kernels: 14.5 us -> 14.7 us  [the longest x1 13.7 us: rotate(): pl.pallas_call(rotate_kernel, out_shape=(jax.ShapeDtypeStruct((rows, 128)...]
  transfers between devices with their start and end apart: 2 -> 3, of which waited for: 1 -> 2; matrix products, arithmetic and copies ran while one was open for 1% -> 0% of each run, Pallas kernels for 9% -> 1%
where the time goes in v3:
time: 122 us
  blocking collectives  73.4 us (60%)
  starting transfers between devices  17 us (14%)
  Pallas kernels  15.1 us (12%)
  between operations  14.1 us (12%)
  waiting for transfers between devices  2 us (2%)
    all_to_all x6, blocking collectives, exchange(): return lax.all_to_all(parts, axis, 0, 0, tiled=True)  73.4 us
    ppermute x2, starting transfers between devices, swap_cores(): return lax.ppermute(value, 'core', ((0, 1), (1, 0)))  17 us
    pallas_call x1, Pallas kernels, rotate(): pl.pallas_call(rotate_kernel, out_shape=(jax.ShapeDtypeStruct((rows, 128)...  13.7 us
  transfers between devices with their start and end apart: 3, of which 2 were waited for; matrix products, arithmetic and copies ran while one was open for 0% of the time, Pallas kernels for 1%

profile of v3, /device:TPU:1, one launch (start us, length us, event | category | flops | bytes accessed | tf_op | source)
XLA Modules:
  0.0 121.9 jit_solution(5792094188968981416)
XLA Ops:
  7.2 0.0 all-gather.3.cloned.1.call-start
  7.2 0.0 copy-start
  7.2 14.6 %all_to_all.30.m_ref = f32[4,512,128]{2,1,0:T(8,128)S(1)} all-to-all(f32[4,512,128]{2,1,0:T(8,128)} %bitcast.10), channel_id=1, replica_groups=mesh['z'=8,'y'=8,'core'=2,'x'=4] {'x'}, dimensions={0} | all-to-all | bytes 2097152 | tf_op jit(solution)/shard_map/all_to_all | solution.py:266
  21.8 0.0 all-gather.3.cloned.1.call-update
  21.8 1.1 shard_map.41
  22.9 8.6 %collective-permute-start = (f32[5,128,128]{2,1,0:T(8,128)S(1)}, f32[5,128,128]{2,1,0:T(8,128)S(1)}, u32[]{:S(2)}, u32[]{:S(2)}) collective-permute-start(f32[5,128,128]{2,1,0:T(8,128)S(1)} %get-tuple-element.12), channel_id=1, source_target_pairs={{0,4},{4,0},{1,5},{5,1},{2,6},{6,2},{3,7},{7,3},{8,12},{12,8},{9,1... | collective-permute-start | bytes 983048 | tf_op jit(solution)/shard_map/ppermute | solution.py:279
  31.5 1.2 %collective-permute-done = f32[5,128,128]{2,1,0:T(8,128)S(1)} collective-permute-done((f32[5,128,128]{2,1,0:T(8,128)S(1)}, f32[5,128,128]{2,1,0:T(8,128)S(1)}, u32[]{:S(2)}, u32[]{:S(2)}) %collective-permute-start) | collective-permute-done | bytes 327712 | tf_op jit(solution)/shard_map/ppermute | solution.py:279
  32.8 9.2 %all_to_all.31 = f32[4,160,128]{2,1,0:T(8,128)S(1)} all-to-all(f32[4,160,128]{2,1,0:T(8,128)S(1)} %bitcast.11), channel_id=1, replica_groups=mesh['z'=8,'y'=8,'core'=2,'x'=4] {'x'}, dimensions={0} | all-to-all | bytes 655360 | tf_op jit(solution)/shard_map/all_to_all | solution.py:266
  42.0 13.9 %all_to_all.32 = f32[8,20,128]{2,1,0:T(8,128)S(1)} all-to-all(f32[8,20,128]{2,1,0:T(8,128)S(1)} %reshape.17), channel_id=1, replica_groups=mesh['z'=8,'y'=8,'core'=2,'x'=4] {'y'}, dimensions={0} | all-to-all | bytes 163840 | tf_op jit(solution)/shard_map/all_to_all | solution.py:266
  55.9 17.5 %all_to_all.33 = f32[8,20,128]{2,1,0:T(8,128)S(1)} all-to-all(f32[8,20,128]{2,1,0:T(8,128)S(1)} %broadcast_in_dim.8), channel_id=1, replica_groups=mesh['z'=8,'y'=8,'core'=2,'x'=4] {'z'}, dimensions={0} | all-to-all | bytes 163840 | tf_op jit(solution)/shard_map/all_to_all | solution.py:266
  73.5 10.0 %all_to_all.34 = f32[8,20,128]{2,1,0:T(8,128)S(1)} all-to-all(f32[8,20,128]{2,1,0:T(8,128)S(1)} %broadcast_in_dim.9), channel_id=1, replica_groups=mesh['z'=8,'y'=8,'core'=2,'x'=4] {'y'}, dimensions={0} | all-to-all | bytes 163840 | tf_op jit(solution)/shard_map/all_to_all | solution.py:266
  83.5 8.3 %all_to_all.35 = f32[4,160,128]{2,1,0:T(8,128)S(1)} all-to-all(f32[4,160,128]{2,1,0:T(8,128)S(1)} %broadcast_in_dim.22), channel_id=1, replica_groups=mesh['z'=8,'y'=8,'core'=2,'x'=4] {'x'}, dimensions={0} | all-to-all | bytes 655360 | tf_op jit(solution)/shard_map/all_to_all | solution.py:266
  91.7 8.4 %collective-permute-start.1 = (f32[5,128,128]{2,1,0:T(8,128)S(1)}, f32[5,128,128]{2,1,0:T(8,128)S(1)}, u32[]{:S(2)}, u32[]{:S(2)}) collective-permute-start(f32[5,128,128]{2,1,0:T(8,128)S(1)} %bitcast.7), channel_id=1, source_target_pairs={{0,4},{4,0},{1,5},{5,1},{2,6},{6,2},{3,7},{7,3},{8,12},{12,8},{9,1... | collective-permute-start | bytes 983048 | tf_op jit(solution)/shard_map/ppermute | solution.py:279
  100.1 0.0 copy-done
  100.1 0.4 shard_map.42
  100.5 0.1 pad_add_fusion.place_ref
  100.6 0.7 collective-permute-done.1.other_ref
  101.4 0.0 all-gather.3.cloned.1.call-done
  101.4 13.7 %shard_map.43 = (f32[2048,128]{1,0:T(8,128)}, f32[1,128]{1,0:T(1,128)}) custom-call(s32[2]{0:T(128)S(1)} %pad_add_fusion.place_ref, f32[5,128,128]{2,1,0:T(8,128)S(1)} %bitcast.8, f32[5,128,128]{2,1,0:T(8,128)S(1)} %collective-permute-done.1.other_ref, bf16[2,256,256]{2,1,0:T(8,128)(2,1)S(1)} %get-tuple-element.13.start_ref, ...), custom_call_target="tpu_custom_call" | custom-call | tf_op jit(solution)/shard_map/pallas_call | solution.py:197
  (9 shorter events, 0.1 us)
Async XLA Ops:
  7.2 94.2 %all-gather.3.cloned.1.call-start = ((), (), s32[]{:S(2)}) async-start(), calls=%async_computation.6 | async-start | bytes 5242880 | tf_op jit(solution)/shard_map/all_gather | solution.py:287
  7.2 92.9 %copy-start = (s32[2,256]{1,0:T(2,128)S(1)}, s32[2,256]{1,0:T(2,128)}, u32[]{:S(2)}) copy-start(s32[2,256]{1,0:T(2,128)} %order_ref.1) | copy-start | bytes 6148
  22.9 9.8 %collective-permute-start = (f32[5,128,128]{2,1,0:T(8,128)S(1)}, f32[5,128,128]{2,1,0:T(8,128)S(1)}, u32[]{:S(2)}, u32[]{:S(2)}) collective-permute-start(f32[5,128,128]{2,1,0:T(8,128)S(1)} %get-tuple-element.12), channel_id=1, source_target_pairs={{0,4},{4,0},{1,5},{5,1},{2,6},{6,2},{3,7},{7,3},{8,12},{12,8},{9,1... | collective-permute-start | bytes 983048 | tf_op jit(solution)/shard_map/ppermute | solution.py:279
  91.7 9.7 %collective-permute-start.1 = (f32[5,128,128]{2,1,0:T(8,128)S(1)}, f32[5,128,128]{2,1,0:T(8,128)S(1)}, u32[]{:S(2)}, u32[]{:S(2)}) collective-permute-start(f32[5,128,128]{2,1,0:T(8,128)S(1)} %bitcast.7), channel_id=1, source_target_pairs={{0,4},{4,0},{1,5},{5,1},{2,6},{6,2},{3,7},{7,3},{8,12},{12,8},{9,1... | collective-permute-start | bytes 983048 | tf_op jit(solution)/shard_map/ppermute | solution.py:279
Sparse Core Ops, SparseCore 0:
  22.0 62.0 all-gather.2

commit v4 on v3

--- a/solution.py
+++ b/solution.py
@@ -262,17 +262,17 @@
     )(core_index, blocks)
 
 
-def exchange(parts, axis):
-    return lax.all_to_all(parts, axis, 0, 0, tiled=True)
-
-
-def sum_part(value, axis):
-    count = lax.axis_size(axis)
-    return exchange(value.reshape(count, value.shape[0] // count, 128), axis).sum(0)
-
-
-def collect(value, axis):
-    return exchange(jnp.broadcast_to(value[None], (lax.axis_size(axis), *value.shape)), axis)
+def exchange(parts, axes):
+    return lax.all_to_all(parts, axes, 0, 0, tiled=True)
+
+
+def sum_part(value, axes):
+    count = lax.axis_size(axes)
+    return exchange(value.reshape(count, value.shape[0] // count, 128), axes).sum(0)
+
+
+def collect(value, axes):
+    return exchange(jnp.broadcast_to(value[None], (lax.axis_size(axes), *value.shape)), axes)
 
 
 def swap_cores(value):
@@ -287,12 +287,8 @@
     whole = lax.all_gather(matrix, "x")
     mine, theirs = grams(place[1:], blocks)
     gram = (mine + swap_cores(theirs)).reshape(640, 128)
-    for axis in ("x", "y"):
-        gram = sum_part(gram, axis)
-    gram = collect(gram, "z").sum(0)
-    for axis in ("y", "x"):
-        gram = collect(gram, axis).reshape(-1, 128)
-    own = gram.reshape(5, 128, 128)
+    gram = collect(sum_part(gram, ("y", "x")), "z").sum(0)
+    own = collect(gram, ("y", "x")).reshape(5, 128, 128)
     density, rms = rotate(place, own, swap_cores(own), start, end, whole)
     return density, rms.reshape(128)
 

time: 122 us -> 117 us (0.959)
  blocking collectives: 73.4 us -> 69.5 us
    all_to_all x6 -> x4, blocking collectives: 73.4 us -> 69.5 us  [exchange(): return lax.all_to_all(parts, axes, 0, 0, tiled=True)]
    ppermute x2, starting transfers between devices: 17 us -> 15.8 us  [swap_cores(): return lax.ppermute(value, 'core', ((0, 1), (1, 0)))]
where the time goes in v4:
time: 117 us
  blocking collectives  69.5 us (59%)
  starting transfers between devices  15.8 us (14%)
  Pallas kernels  15.1 us (13%)
  between operations  14.1 us (12%)
  waiting for transfers between devices  2 us (2%)
    all_to_all x4, blocking collectives, exchange(): return lax.all_to_all(parts, axes, 0, 0, tiled=True)  69.5 us
    ppermute x2, starting transfers between devices, swap_cores(): return lax.ppermute(value, 'core', ((0, 1), (1, 0)))  15.8 us
    pallas_call x1, Pallas kernels, rotate(): pl.pallas_call(rotate_kernel, out_shape=(jax.ShapeDtypeStruct((rows, 128)...  13.6 us
  transfers between devices with their start and end apart: 3, of which 2 were waited for; matrix products, arithmetic and copies ran while one was open for 0% of the time, Pallas kernels for 1%

profile of v4, /device:TPU:1, one launch (start us, length us, event | category | flops | bytes accessed | tf_op | source)
XLA Modules:
  0.0 116.8 jit_solution(5806288431822819226)
XLA Ops:
  7.2 0.0 all-gather.3.cloned.1.call-start
  7.2 14.6 %all_to_all.20.m_ref = f32[4,512,128]{2,1,0:T(8,128)S(1)} all-to-all(f32[4,512,128]{2,1,0:T(8,128)} %bitcast.6), channel_id=1, replica_groups=mesh['z'=8,'y'=8,'core'=2,'x'=4] {'x'}, dimensions={0} | all-to-all | bytes 2097152 | tf_op jit(solution)/shard_map/all_to_all | solution.py:266
  21.8 0.0 copy-start
  21.8 0.0 all-gather.3.cloned.1.call-update
  21.8 1.1 shard_map.41
  22.9 8.6 %collective-permute-start = (f32[5,128,128]{2,1,0:T(8,128)S(1)}, f32[5,128,128]{2,1,0:T(8,128)S(1)}, u32[]{:S(2)}, u32[]{:S(2)}) collective-permute-start(f32[5,128,128]{2,1,0:T(8,128)S(1)} %get-tuple-element.12), channel_id=1, source_target_pairs={{0,4},{4,0},{1,5},{5,1},{2,6},{6,2},{3,7},{7,3},{8,12},{12,8},{9,1... | collective-permute-start | bytes 983048 | tf_op jit(solution)/shard_map/ppermute | solution.py:279
  31.5 1.2 %collective-permute-done = f32[5,128,128]{2,1,0:T(8,128)S(1)} collective-permute-done((f32[5,128,128]{2,1,0:T(8,128)S(1)}, f32[5,128,128]{2,1,0:T(8,128)S(1)}, u32[]{:S(2)}, u32[]{:S(2)}) %collective-permute-start) | collective-permute-done | bytes 327712 | tf_op jit(solution)/shard_map/ppermute | solution.py:279
  32.8 21.1 %all_to_all.21 = f32[32,20,128]{2,1,0:T(8,128)S(1)} all-to-all(f32[32,20,128]{2,1,0:T(8,128)S(1)} %reshape_reshape.3), channel_id=1, replica_groups=mesh['z'=8,'y'=8,'core'=2,'x'=4] {'y','x'}, dimensions={0} | all-to-all | bytes 655360 | tf_op jit(solution)/shard_map/all_to_all | solution.py:266
  54.0 17.4 %all_to_all.22 = f32[8,20,128]{2,1,0:T(8,128)S(1)} all-to-all(f32[8,20,128]{2,1,0:T(8,128)S(1)} %broadcast_in_dim.4), channel_id=1, replica_groups=mesh['z'=8,'y'=8,'core'=2,'x'=4] {'z'}, dimensions={0} | all-to-all | bytes 163840 | tf_op jit(solution)/shard_map/all_to_all | solution.py:266
  71.4 16.3 %all_to_all.23 = f32[32,20,128]{2,1,0:T(8,128)S(1)} all-to-all(f32[32,20,128]{2,1,0:T(8,128)S(1)} %broadcast_in_dim.5), channel_id=1, replica_groups=mesh['z'=8,'y'=8,'core'=2,'x'=4] {'y','x'}, dimensions={0} | all-to-all | bytes 655360 | tf_op jit(solution)/shard_map/all_to_all | solution.py:266
  87.8 7.2 %collective-permute-start.1 = (f32[5,128,128]{2,1,0:T(8,128)S(1)}, f32[5,128,128]{2,1,0:T(8,128)S(1)}, u32[]{:S(2)}, u32[]{:S(2)}) collective-permute-start(f32[5,128,128]{2,1,0:T(8,128)S(1)} %reshape.16.own_ref), channel_id=1, source_target_pairs={{0,4},{4,0},{1,5},{5,1},{2,6},{6,2},{3,7},{7,3},{8,12},{12,8},{9,1... | collective-permute-start | bytes 983048 | tf_op jit(solution)/shard_map/ppermute | solution.py:279
  95.0 0.0 copy-done
  95.0 0.4 shard_map.42
  95.4 0.1 pad_add_fusion.place_ref
  95.5 0.7 collective-permute-done.1.other_ref
  96.2 0.0 all-gather.3.cloned.1.call-done
  96.2 13.6 %shard_map.43 = (f32[2048,128]{1,0:T(8,128)}, f32[1,128]{1,0:T(1,128)}) custom-call(s32[2]{0:T(128)S(1)} %pad_add_fusion.place_ref, f32[5,128,128]{2,1,0:T(8,128)S(1)} %reshape.16.own_ref, f32[5,128,128]{2,1,0:T(8,128)S(1)} %collective-permute-done.1.other_ref, bf16[2,256,256]{2,1,0:T(8,128)(2,1)S(1)} %get-tuple-element.13.start_ref, ...), custom_call_target="tpu_custom_call" | custom-call | tf_op jit(solution)/shard_map/pallas_call | solution.py:197
  (7 shorter events, 0.2 us)
Async XLA Ops:
  7.2 89.1 %all-gather.3.cloned.1.call-start = ((), (), s32[]{:S(2)}) async-start(), calls=%async_computation.4 | async-start | bytes 5242880 | tf_op jit(solution)/shard_map/all_gather | solution.py:287
  21.8 73.2 %copy-start = (s32[2,256]{1,0:T(2,128)S(1)}, s32[2,256]{1,0:T(2,128)}, u32[]{:S(2)}) copy-start(s32[2,256]{1,0:T(2,128)} %order_ref.1) | copy-start | bytes 6148
  22.9 9.8 %collective-permute-start = (f32[5,128,128]{2,1,0:T(8,128)S(1)}, f32[5,128,128]{2,1,0:T(8,128)S(1)}, u32[]{:S(2)}, u32[]{:S(2)}) collective-permute-start(f32[5,128,128]{2,1,0:T(8,128)S(1)} %get-tuple-element.12), channel_id=1, source_target_pairs={{0,4},{4,0},{1,5},{5,1},{2,6},{6,2},{3,7},{7,3},{8,12},{12,8},{9,1... | collective-permute-start | bytes 983048 | tf_op jit(solution)/shard_map/ppermute | solution.py:279
  87.8 8.4 %collective-permute-start.1 = (f32[5,128,128]{2,1,0:T(8,128)S(1)}, f32[5,128,128]{2,1,0:T(8,128)S(1)}, u32[]{:S(2)}, u32[]{:S(2)}) collective-permute-start(f32[5,128,128]{2,1,0:T(8,128)S(1)} %reshape.16.own_ref), channel_id=1, source_target_pairs={{0,4},{4,0},{1,5},{5,1},{2,6},{6,2},{3,7},{7,3},{8,12},{12,8},{9,1... | collective-permute-start | bytes 983048 | tf_op jit(solution)/shard_map/ppermute | solution.py:279
Sparse Core Ops, SparseCore 0:
  22.0 67.4 all-gather.2

commit v5 on v4

--- a/solution.py
+++ b/solution.py
@@ -268,7 +268,7 @@
 
 def sum_part(value, axes):
     count = lax.axis_size(axes)
-    return exchange(value.reshape(count, value.shape[0] // count, 128), axes).sum(0)
+    return exchange(value.reshape(count, 1, value.size // count), axes).sum(0)
 
 
 def collect(value, axes):

time: 117 us -> 114 us (0.974)
  blocking collectives: 69.5 us -> 67.3 us
    all_to_all x4, blocking collectives: 69.5 us -> 67.3 us  [exchange(): return lax.all_to_all(parts, axes, 0, 0, tiled=True)]
  transfers between devices with their start and end apart: 3 -> 3, of which waited for: 2 -> 2; matrix products, arithmetic and copies ran while one was open for 0% -> 1% of each run, Pallas kernels for 1% -> 1%
where the time goes in v5:
time: 114 us
  blocking collectives  67.3 us (59%)
  Pallas kernels  15.1 us (13%)
  starting transfers between devices  14.9 us (13%)
  between operations  14.1 us (12%)
  waiting for transfers between devices  2 us (2%)
    all_to_all x4, blocking collectives, exchange(): return lax.all_to_all(parts, axes, 0, 0, tiled=True)  67.3 us
    ppermute x2, starting transfers between devices, swap_cores(): return lax.ppermute(value, 'core', ((0, 1), (1, 0)))  14.9 us
    pallas_call x1, Pallas kernels, rotate(): pl.pallas_call(rotate_kernel, out_shape=(jax.ShapeDtypeStruct((rows, 128)...  13.7 us
  transfers between devices with their start and end apart: 3, of which 2 were waited for; matrix products, arithmetic and copies ran while one was open for 1% of the time, Pallas kernels for 1%

profile of v5, /device:TPU:1, one launch (start us, length us, event | category | flops | bytes accessed | tf_op | source)
XLA Modules:
  0.0 114.1 jit_solution(4566062631025200045)
XLA Ops:
  7.2 0.0 copy-start
  7.2 0.0 all-gather.3.cloned.1.call-start
  7.2 14.6 %all_to_all.20.m_ref = f32[4,512,128]{2,1,0:T(8,128)S(1)} all-to-all(f32[4,512,128]{2,1,0:T(8,128)} %bitcast.10), channel_id=1, replica_groups=mesh['z'=8,'y'=8,'core'=2,'x'=4] {'x'}, dimensions={0} | all-to-all | bytes 2097152 | tf_op jit(solution)/shard_map/all_to_all | solution.py:266
  21.8 0.0 all-gather.3.cloned.1.call-update
  21.8 1.1 shard_map.41
  22.9 8.6 %collective-permute-start = (f32[5,128,128]{2,1,0:T(8,128)S(1)}, f32[5,128,128]{2,1,0:T(8,128)S(1)}, u32[]{:S(2)}, u32[]{:S(2)}) collective-permute-start(f32[5,128,128]{2,1,0:T(8,128)S(1)} %get-tuple-element.12), channel_id=1, source_target_pairs={{0,4},{4,0},{1,5},{5,1},{2,6},{6,2},{3,7},{7,3},{8,12},{12,8},{9,1... | collective-permute-start | bytes 983048 | tf_op jit(solution)/shard_map/ppermute | solution.py:279
  31.5 1.2 %collective-permute-done = f32[5,128,128]{2,1,0:T(8,128)S(1)} collective-permute-done((f32[5,128,128]{2,1,0:T(8,128)S(1)}, f32[5,128,128]{2,1,0:T(8,128)S(1)}, u32[]{:S(2)}, u32[]{:S(2)}) %collective-permute-start) | collective-permute-done | bytes 327712 | tf_op jit(solution)/shard_map/ppermute | solution.py:279
  32.8 20.0 %all_to_all.21 = f32[32,1,2560]{2,1,0:T(1,128)S(1)} all-to-all(f32[32,1,2560]{2,1,0:T(1,128)S(1)} %bitcast.11), channel_id=1, replica_groups=mesh['z'=8,'y'=8,'core'=2,'x'=4] {'y','x'}, dimensions={0} | all-to-all | bytes 655360 | tf_op jit(solution)/shard_map/all_to_all | solution.py:266
  52.8 0.2 reduce_sum.18
  53.0 17.2 %all_to_all.22 = f32[8,1,2560]{2,1,0:T(1,128)S(1)} all-to-all(f32[8,1,2560]{2,1,0:T(1,128)S(1)} %broadcast_in_dim.4), channel_id=1, replica_groups=mesh['z'=8,'y'=8,'core'=2,'x'=4] {'z'}, dimensions={0} | all-to-all | bytes 163840 | tf_op jit(solution)/shard_map/all_to_all | solution.py:266
  70.3 0.1 reduce_sum.19
  70.3 0.2 broadcast_in_dim.5
  70.5 15.5 %all_to_all.23 = f32[32,1,2560]{2,1,0:T(1,128)S(1)} all-to-all(f32[32,1,2560]{2,1,0:T(1,128)S(1)} %broadcast_in_dim.5), channel_id=1, replica_groups=mesh['z'=8,'y'=8,'core'=2,'x'=4] {'y','x'}, dimensions={0} | all-to-all | bytes 655360 | tf_op jit(solution)/shard_map/all_to_all | solution.py:266
  86.0 6.3 %collective-permute-start.1 = (f32[5,128,128]{2,1,0:T(8,128)S(1)}, f32[5,128,128]{2,1,0:T(8,128)S(1)}, u32[]{:S(2)}, u32[]{:S(2)}) collective-permute-start(f32[5,128,128]{2,1,0:T(8,128)S(1)} %bitcast.7), channel_id=1, source_target_pairs={{0,4},{4,0},{1,5},{5,1},{2,6},{6,2},{3,7},{7,3},{8,12},{12,8},{9,1... | collective-permute-start | bytes 983048 | tf_op jit(solution)/shard_map/ppermute | solution.py:279
  92.3 0.0 copy-done
  92.3 0.4 shard_map.42
  92.7 0.1 pad_add_fusion.place_ref
  92.8 0.7 collective-permute-done.1.other_ref
  93.5 0.0 all-gather.3.cloned.1.call-done
  93.5 13.7 %shard_map.43 = (f32[2048,128]{1,0:T(8,128)}, f32[1,128]{1,0:T(1,128)}) custom-call(s32[2]{0:T(128)S(1)} %pad_add_fusion.place_ref, f32[5,128,128]{2,1,0:T(8,128)S(1)} %bitcast.8, f32[5,128,128]{2,1,0:T(8,128)S(1)} %collective-permute-done.1.other_ref, bf16[2,256,256]{2,1,0:T(8,128)(2,1)S(1)} %get-tuple-element.13.start_ref, ...), custom_call_target="tpu_custom_call" | custom-call | tf_op jit(solution)/shard_map/pallas_call | solution.py:197
  (2 shorter events, 0.1 us)
Async XLA Ops:
  7.2 85.1 %copy-start = (s32[2,256]{1,0:T(2,128)S(1)}, s32[2,256]{1,0:T(2,128)}, u32[]{:S(2)}) copy-start(s32[2,256]{1,0:T(2,128)} %order_ref.1) | copy-start | bytes 6148
  7.2 86.4 %all-gather.3.cloned.1.call-start = ((), (), s32[]{:S(2)}) async-start(), calls=%async_computation.4 | async-start | bytes 5242880 | tf_op jit(solution)/shard_map/all_gather | solution.py:287
  22.9 9.8 %collective-permute-start = (f32[5,128,128]{2,1,0:T(8,128)S(1)}, f32[5,128,128]{2,1,0:T(8,128)S(1)}, u32[]{:S(2)}, u32[]{:S(2)}) collective-permute-start(f32[5,128,128]{2,1,0:T(8,128)S(1)} %get-tuple-element.12), channel_id=1, source_target_pairs={{0,4},{4,0},{1,5},{5,1},{2,6},{6,2},{3,7},{7,3},{8,12},{12,8},{9,1... | collective-permute-start | bytes 983048 | tf_op jit(solution)/shard_map/ppermute | solution.py:279
  86.0 7.6 %collective-permute-start.1 = (f32[5,128,128]{2,1,0:T(8,128)S(1)}, f32[5,128,128]{2,1,0:T(8,128)S(1)}, u32[]{:S(2)}, u32[]{:S(2)}) collective-permute-start(f32[5,128,128]{2,1,0:T(8,128)S(1)} %bitcast.7), channel_id=1, source_target_pairs={{0,4},{4,0},{1,5},{5,1},{2,6},{6,2},{3,7},{7,3},{8,12},{12,8},{9,1... | collective-permute-start | bytes 983048 | tf_op jit(solution)/shard_map/ppermute | solution.py:279
Sparse Core Ops, SparseCore 0:
  22.0 66.1 all-gather.2

commit v6 on v5

--- a/solution.py
+++ b/solution.py
@@ -12,7 +12,7 @@
 NN = (((1,), (0,)), ((), ()))
 NT = (((1,), (1,)), ((), ()))
 TN = (((0,), (0,)), ((), ()))
-PAIRS = ((0, 0), (0, 1), (1, 1), (2, 2), (2, 3), (3, 3), (0, 2), (0, 3), (1, 2), (1, 3))
+HALF_ROWS = 544
 LIMIT = pltpu.CompilerParams(vmem_limit_bytes=48 * 1024 * 1024)
 VMEM = pl.BlockSpec(memory_space=pltpu.VMEM)
 SMEM = pl.BlockSpec(memory_space=pltpu.SMEM)
@@ -127,8 +127,8 @@
         fetch.append(pltpu.make_async_copy(whole_ref.at[:, rows, :], held_rows.at[i], in_sems.at[i]))
         fetch[-1].start()
     core = place_ref[1]
-    g_ref[pl.ds(5 * core, 5)] = own_ref[...]
-    g_ref[pl.ds(5 * (1 - core), 5)] = other_ref[...]
+    g_ref[core] = own_ref[:520, :]
+    g_ref[1 - core] = other_ref[:520, :]
     own_pair, own_side = place_ref[0] % 2, place_ref[0] // 2
     half = pl.ds(pl.multiple_of(128 * own_pair, 128), 128)
 
@@ -157,16 +157,25 @@
         sides = [jnp.concatenate([xa[a, side, lane] for lane in lanes], axis=1) for side in range(2)]
         return jnp.concatenate(sides, axis=0)
 
+    def unpack(i):
+        row = lax.broadcasted_iota(jnp.int32, (128, 128), 0)
+        col = lax.broadcasted_iota(jnp.int32, (128, 128), 1)
+        packed = g_ref[i, :128, :]
+        turned = packed.T
+        one = jnp.where(row <= col, packed, turned)
+        other = jnp.where(row > col, packed, jnp.where(row == col, g_ref[i, 512:513, :], turned))
+        return square(one, g_ref[i, 128:256, :], other)
+
     def square(a, b, d):
         return jnp.concatenate([jnp.concatenate([a, b], axis=1), jnp.concatenate([b.T, d], axis=1)], axis=0)
 
-    solve([square(g_ref[i], g_ref[i + 1], g_ref[i + 2]) for i in (0, 3)], 0)
+    solve([unpack(i) for i in range(2)], 0)
     end = end_ref[0, half, :]
     both = [pick(end, placed(a, range(4))) for a in range(2)]
     basis = [value[:, :256] for value in both]
     turned = [dot(value[:, :256], value[:, 256:], NT) for value in both]
     between = jnp.concatenate(
-        [jnp.concatenate([g_ref[6], g_ref[7]], axis=1), jnp.concatenate([g_ref[8], g_ref[9]], axis=1)], axis=0
+        [jnp.concatenate([g_ref[i, 256:384, :], g_ref[i, 384:512, :]], axis=1) for i in range(2)], axis=0
     )
     cross = dot(dot(basis[0], between), basis[1], NT)
     solve([square(turned[0], cross, turned[1])], 1)
@@ -203,7 +212,7 @@
         in_specs=[SMEM, VMEM, VMEM, VMEM, VMEM, HBM],
         out_specs=[HBM, VMEM],
         scratch_shapes=[
-            pltpu.VMEM((10, 128, 128), jnp.float32),
+            pltpu.VMEM((2, 520, 128), jnp.float32),
             pltpu.VMEM((2, 2, 4, 128, 128), jnp.float32),
             pltpu.VMEM((2, 2, 4, 128, 128), jnp.float32),
             pltpu.VMEM((2, 2, 128, 128), jnp.float32),
@@ -238,24 +247,33 @@
         return short_dot(lh, rh, TN) + small
 
     low, high = slice(0, 128), slice(128, 256)
-    blocks = []
-    for part in parts:
+    between = product(*parts)
+    row = lax.broadcasted_iota(jnp.int32, (128, 128), 0)
+    col = lax.broadcasted_iota(jnp.int32, (128, 128), 1)
+    halves = []
+    for i, part in enumerate(parts):
         whole = product(part, part)
-        blocks += [whole[low, low], whole[low, high], whole[high, high]]
-    between = product(*parts)
-    blocks += [between[low, low], between[low, high], between[high, low], between[high, high]]
-    for core, halves in enumerate(((mine_ref, theirs_ref), (theirs_ref, mine_ref))):
+        own = (low, high)[i]
+        diag = jnp.sum(jnp.where(row == col, whole[high, high], 0.0), axis=0, keepdims=True)
+        packed = jnp.where(row <= col, whole[low, low], whole[high, high])
+        blocks = [packed, whole[low, high], between[own, low], between[own, high]]
+        rest = jnp.zeros((HALF_ROWS - 520, 128), jnp.float32)
+        halves.append([*blocks, jnp.broadcast_to(diag, (8, 128)), rest])
+    for core in range(2):
 
         @pl.when(core_ref[0] == core)
-        def _(halves=halves):
-            for i, block in enumerate(blocks):
-                halves[i // 5][i % 5] = block
+        def _(core=core):
+            for ref, half in ((mine_ref, halves[core]), (theirs_ref, halves[1 - core])):
+                at = 0
+                for block in half:
+                    ref[at : at + block.shape[0], :] = block
+                    at += block.shape[0]
 
 
 def grams(core_index, blocks):
     return pl.pallas_call(
         gram_kernel,
-        out_shape=(jax.ShapeDtypeStruct((5, 128, 128), jnp.float32),) * 2,
+        out_shape=(jax.ShapeDtypeStruct((HALF_ROWS, 128), jnp.float32),) * 2,
         in_specs=[SMEM, VMEM],
         out_specs=[VMEM, VMEM],
         compiler_params=LIMIT,
@@ -286,9 +304,9 @@
     matrix, blocks = lax.optimization_barrier((matrix, blocks))
     whole = lax.all_gather(matrix, "x")
     mine, theirs = grams(place[1:], blocks)
-    gram = (mine + swap_cores(theirs)).reshape(640, 128)
+    gram = mine + swap_cores(theirs)
     gram = collect(sum_part(gram, ("y", "x")), "z").sum(0)
-    own = collect(gram, ("y", "x")).reshape(5, 128, 128)
+    own = collect(gram, ("y", "x")).reshape(HALF_ROWS, 128)
     density, rms = rotate(place, own, swap_cores(own), start, end, whole)
     return density, rms.reshape(128)
 

time: 114 us -> 113 us (level)
  blocking collectives: 67.3 us -> 66 us
    all_to_all x4, blocking collectives: 67.3 us -> 66 us  [exchange(): return lax.all_to_all(parts, axes, 0, 0, tiled=True)]
  transfers between devices with their start and end apart: 3 -> 3, of which waited for: 2 -> 2; matrix products, arithmetic and copies ran while one was open for 1% -> 0% of each run, Pallas kernels for 1% -> 1%
where the time goes in v6:
time: 113 us; the launch traced here: 112 us
  blocking collectives  66 us (58%)
  Pallas kernels  15.2 us (13%)
  starting transfers between devices  14.6 us (13%)
  between operations  14.1 us (12%)
  waiting for transfers between devices  1.86 us (2%)
    all_to_all x4, blocking collectives, exchange(): return lax.all_to_all(parts, axes, 0, 0, tiled=True)  66 us
    ppermute x2, starting transfers between devices, swap_cores(): return lax.ppermute(value, 'core', ((0, 1), (1, 0)))  14.6 us
    pallas_call x1, Pallas kernels, rotate(): pl.pallas_call(rotate_kernel, out_shape=(jax.ShapeDtypeStruct((rows, 128)...  13.7 us
  transfers between devices with their start and end apart: 3, of which 2 were waited for; matrix products, arithmetic and copies ran while one was open for 0% of the time, Pallas kernels for 1%

profile of v6, /device:TPU:1, one launch (start us, length us, event | category | flops | bytes accessed | tf_op | source)
XLA Modules:
  0.0 112.2 jit_solution(509163097125790315)
XLA Ops:
  7.2 0.0 copy-start
  7.2 0.0 all-gather.3.cloned.1.call-start
  7.2 14.6 %all_to_all.20.m_ref = f32[4,512,128]{2,1,0:T(8,128)S(1)} all-to-all(f32[4,512,128]{2,1,0:T(8,128)} %bitcast.10), channel_id=1, replica_groups=mesh['z'=8,'y'=8,'core'=2,'x'=4] {'x'}, dimensions={0} | all-to-all | bytes 2097152 | tf_op jit(solution)/shard_map/all_to_all | solution.py:284
  21.8 0.0 all-gather.3.cloned.1.call-update
  21.8 1.1 shard_map.41
  22.9 8.6 %collective-permute-start = (f32[544,128]{1,0:T(8,128)S(1)}, f32[544,128]{1,0:T(8,128)S(1)}, u32[]{:S(2)}, u32[]{:S(2)}) collective-permute-start(f32[544,128]{1,0:T(8,128)S(1)} %get-tuple-element.12), channel_id=1, source_target_pairs={{0,4},{4,0},{1,5},{5,1},{2,6},{6,2},{3,7},{7,3},{8,12},{12,8},{9,1... | collective-permute-start | bytes 835592 | tf_op jit(solution)/shard_map/ppermute | solution.py:297
  31.5 1.2 %collective-permute-done = f32[544,128]{1,0:T(8,128)S(1)} collective-permute-done((f32[544,128]{1,0:T(8,128)S(1)}, f32[544,128]{1,0:T(8,128)S(1)}, u32[]{:S(2)}, u32[]{:S(2)}) %collective-permute-start) | collective-permute-done | bytes 278560 | tf_op jit(solution)/shard_map/ppermute | solution.py:297
  32.7 19.3 %all_to_all.21 = f32[32,1,2176]{2,1,0:T(1,128)S(1)} all-to-all(f32[32,1,2176]{2,1,0:T(1,128)S(1)} %bitcast.11), channel_id=1, replica_groups=mesh['z'=8,'y'=8,'core'=2,'x'=4] {'y','x'}, dimensions={0} | all-to-all | bytes 557056 | tf_op jit(solution)/shard_map/all_to_all | solution.py:284
  52.0 0.2 reduce_sum.18
  52.2 17.1 %all_to_all.22 = f32[8,1,2176]{2,1,0:T(1,128)S(1)} all-to-all(f32[8,1,2176]{2,1,0:T(1,128)S(1)} %broadcast_in_dim.4), channel_id=1, replica_groups=mesh['z'=8,'y'=8,'core'=2,'x'=4] {'z'}, dimensions={0} | all-to-all | bytes 139264 | tf_op jit(solution)/shard_map/all_to_all | solution.py:284
  69.3 0.1 reduce_sum.19
  69.3 0.1 broadcast_in_dim.5
  69.5 15.0 %all_to_all.23 = f32[32,1,2176]{2,1,0:T(1,128)S(1)} all-to-all(f32[32,1,2176]{2,1,0:T(1,128)S(1)} %broadcast_in_dim.5), channel_id=1, replica_groups=mesh['z'=8,'y'=8,'core'=2,'x'=4] {'y','x'}, dimensions={0} | all-to-all | bytes 557056 | tf_op jit(solution)/shard_map/all_to_all | solution.py:284
  84.5 6.0 %collective-permute-start.1 = (f32[544,128]{1,0:T(8,128)S(1)}, f32[544,128]{1,0:T(8,128)S(1)}, u32[]{:S(2)}, u32[]{:S(2)}) collective-permute-start(f32[544,128]{1,0:T(8,128)S(1)} %bitcast.7), channel_id=1, source_target_pairs={{0,4},{4,0},{1,5},{5,1},{2,6},{6,2},{3,7},{7,3},{8,12},{12,8},{9,1... | collective-permute-start | bytes 835592 | tf_op jit(solution)/shard_map/ppermute | solution.py:297
  90.5 0.0 copy-done
  90.5 0.4 shard_map.42
  90.9 0.1 pad_add_fusion.place_ref
  91.0 0.7 collective-permute-done.1.other_ref
  91.6 0.0 all-gather.3.cloned.1.call-done
  91.6 13.7 %shard_map.43 = (f32[2048,128]{1,0:T(8,128)}, f32[1,128]{1,0:T(1,128)}) custom-call(s32[2]{0:T(128)S(1)} %pad_add_fusion.place_ref, f32[544,128]{1,0:T(8,128)S(1)} %bitcast.8, f32[544,128]{1,0:T(8,128)S(1)} %collective-permute-done.1.other_ref, bf16[2,256,256]{2,1,0:T(8,128)(2,1)S(1)} %get-tuple-element.13.start_ref, ...), custom_call_target="tpu_custom_call" | custom-call | tf_op jit(solution)/shard_map/pallas_call | solution.py:206
  (2 shorter events, 0.1 us)
Async XLA Ops:
  7.2 83.3 %copy-start = (s32[2,256]{1,0:T(2,128)S(1)}, s32[2,256]{1,0:T(2,128)}, u32[]{:S(2)}) copy-start(s32[2,256]{1,0:T(2,128)} %order_ref.1) | copy-start | bytes 6148
  7.2 84.5 %all-gather.3.cloned.1.call-start = ((), (), s32[]{:S(2)}) async-start(), calls=%async_computation.4 | async-start | bytes 5242880 | tf_op jit(solution)/shard_map/all_gather | solution.py:305
  22.9 9.7 %collective-permute-start = (f32[544,128]{1,0:T(8,128)S(1)}, f32[544,128]{1,0:T(8,128)S(1)}, u32[]{:S(2)}, u32[]{:S(2)}) collective-permute-start(f32[544,128]{1,0:T(8,128)S(1)} %get-tuple-element.12), channel_id=1, source_target_pairs={{0,4},{4,0},{1,5},{5,1},{2,6},{6,2},{3,7},{7,3},{8,12},{12,8},{9,1... | collective-permute-start | bytes 835592 | tf_op jit(solution)/shard_map/ppermute | solution.py:297
  84.5 7.2 %collective-permute-start.1 = (f32[544,128]{1,0:T(8,128)S(1)}, f32[544,128]{1,0:T(8,128)S(1)}, u32[]{:S(2)}, u32[]{:S(2)}) collective-permute-start(f32[544,128]{1,0:T(8,128)S(1)} %bitcast.7), channel_id=1, source_target_pairs={{0,4},{4,0},{1,5},{5,1},{2,6},{6,2},{3,7},{7,3},{8,12},{12,8},{9,1... | collective-permute-start | bytes 835592 | tf_op jit(solution)/shard_map/ppermute | solution.py:297
Sparse Core Ops, SparseCore 0:
  22.0 65.6 all-gather.2

commit v7 on v6

v7 whole, which is shorter than its diff:
```python
import jax
import jax.numpy as jnp
from jax import lax
from jax.experimental import pallas as pl
from jax.experimental.pallas import tpu as pltpu
from jax.sharding import Mesh, PartitionSpec as P

ROUNDS = 16
ROWS = 262144
EPS = 1e-06
HIGHEST = lax.Precision.HIGHEST
NN = (((1,), (0,)), ((), ()))
NT = (((1,), (1,)), ((), ()))
TN = (((0,), (0,)), ((), ()))
HALF_ROWS = 544
LIMIT = pltpu.CompilerParams(vmem_limit_bytes=48 * 1024 * 1024)
VMEM = pl.BlockSpec(memory_space=pltpu.VMEM)
SMEM = pl.BlockSpec(memory_space=pltpu.SMEM)
HBM = pl.BlockSpec(memory_space=pltpu.HBM)
CHUNKS = 4


def dot(a, b, dims=NN):
    return lax.dot_general(a, b, dims, precision=HIGHEST, preferred_element_type=jnp.float32)


def short_dot(a, b, dims=NN):
    return lax.dot_general(a, b, dims, preferred_element_type=jnp.float32)


def split(value, count):
    parts = []
    for _ in range(count):
        part = value.astype(jnp.bfloat16)
        value = value - part.astype(jnp.float32)
        parts.append(part)
    return parts


def pick(onehot, value, dims=NN):
    high, mid, low = (short_dot(onehot, part, dims) for part in split(value, 3))
    return high + (mid + low)


def slot_at(place, turn):
    side, inner = place // 128, place % 128
    k = 16 * (inner % 8) + inner // 8
    moved = jnp.where(side == 0, turn + k, turn + 255 - k)
    moved = jnp.where(moved >= 255, moved - 255, moved)
    return jnp.where((side == 0) & (k == 0), 255, moved)


def places_kernel(order_ref, start_ref, end_ref):
    rows = lax.broadcasted_iota(jnp.int32, (256, 256), 0)
    cols = lax.broadcasted_iota(jnp.int32, (256, 256), 1)
    first = (slot_at(rows, 0) == cols).astype(jnp.bfloat16)
    last = (slot_at(rows, ROUNDS) == cols).astype(jnp.bfloat16)
    for step in range(2):
        column_slot = (rows == order_ref[step : step + 1, :]).astype(jnp.bfloat16)
        start_ref[step] = short_dot(first, column_slot, NT).astype(jnp.bfloat16)
        end_ref[step] = short_dot(column_slot, last, NT).astype(jnp.bfloat16)


def rotation(cross, low, high):
    x = high - low
    y = cross + cross
    ax = jnp.abs(x)
    yy = y * y
    hh = x * x + yy + 1e-37
    h = hh * lax.rsqrt(hh)
    w = h + ax
    n = lax.rsqrt(w * w + yy)
    big = w * n
    small = y * n
    gap = h * small * small
    back = x < 0.0
    cs = jnp.where(back, small, big)
    sn = jnp.where(back, big, small)
    return cs, sn, jnp.minimum(low, high) - gap, jnp.maximum(low, high) + gap


def one_round(src, dst, dsrc, ddst, cbuf, sbuf):
    row8 = lax.broadcasted_iota(jnp.int32, (8, 128), 0)
    first, last = row8 == 0, row8 == 7

    def put(tops, bottoms, top, bottom):
        for t in range(15):
            tops[pl.ds(8 * t, 8)] = top[t + 1] if t else jnp.where(first, top[0], top[1])
            bottoms[pl.ds(8 * t + 8, 8)] = bottom[t]
        tops[pl.ds(120, 8)] = jnp.where(last, bottom[15], pltpu.roll(top[0], 7, 0))
        bottoms[pl.ds(0, 8)] = jnp.where(first, top[1], pltpu.roll(bottom[15], 1, 0))

    top, bottom = [], []
    for t in range(16):
        rows = pl.ds(8 * t, 8)
        part = src[0, 0, rows] * src[1, 2, rows] + src[0, 1, rows] * src[1, 3, rows]
        cross = jnp.broadcast_to(jnp.sum(part, axis=1, keepdims=True), (8, 128))
        cs, sn, low, high = rotation(cross, dsrc[0, rows], dsrc[1, rows])
        cbuf[rows] = cs
        sbuf[rows] = sn
        top.append(low)
        bottom.append(high)
    put(ddst.at[0], ddst.at[1], top, bottom)
    for lane in range(4):
        top, bottom = [], []
        for t in range(16):
            rows = pl.ds(8 * t, 8)
            cs, sn = cbuf[rows], sbuf[rows]
            p, q = src[0, lane, rows], src[1, lane, rows]
            top.append(cs * p - sn * q)
            bottom.append(sn * p + cs * q)
        put(dst.at[0, lane], dst.at[1, lane], top, bottom)


TURNING = [
    pltpu.VMEM((2, 4, 128, 128), jnp.float32),
    pltpu.VMEM((2, 4, 128, 128), jnp.float32),
    pltpu.VMEM((2, 128, 128), jnp.float32),
    pltpu.VMEM((2, 128, 128), jnp.float32),
    pltpu.VMEM((128, 128), jnp.float32),
    pltpu.VMEM((128, 128), jnp.float32),
]


def turn(gram, start, xa, xb, da, db, cbuf, sbuf):
    start32 = start.astype(jnp.float32)
    held = pick(start, gram)
    diag = jnp.broadcast_to(jnp.sum(start32 * held, axis=1, keepdims=True), (256, 128))
    for side in range(2):
        rows = slice(128 * side, 128 * side + 128)
        da[side] = diag[rows]
        for lane in range(2):
            cols = slice(128 * lane, 128 * lane + 128)
            xa[side, lane] = start32[rows, cols]
            xa[side, lane + 2] = held[rows, cols]

    def two_rounds(_, carry):
        one_round(xa, xb, da, db, cbuf, sbuf)
        one_round(xb, xa, db, da, cbuf, sbuf)
        return carry

    lax.fori_loop(0, ROUNDS // 2, two_rounds, 0, unroll=True)


def placed(xa, lanes):
    sides = [jnp.concatenate([xa[side, lane] for lane in lanes], axis=1) for side in range(2)]
    return jnp.concatenate(sides, axis=0)


def square(a, b, d):
    return jnp.concatenate([jnp.concatenate([a, b], axis=1), jnp.concatenate([b.T, d], axis=1)], axis=0)


def first_kernel(place_ref, half_ref, start_ref, end_ref, out_ref, *turning):
    row = lax.broadcasted_iota(jnp.int32, (128, 128), 0)
    col = lax.broadcasted_iota(jnp.int32, (128, 128), 1)
    packed = half_ref[:128, :]
    mirrored = packed.T
    one = jnp.where(row <= col, packed, mirrored)
    other = jnp.where(row > col, packed, jnp.where(row == col, half_ref[512:513, :], mirrored))
    turn(square(one, half_ref[128:256, :], other), start_ref[0], *turning)
    own_pair = place_ref[0] % 2
    end = end_ref[0, pl.ds(pl.multiple_of(128 * own_pair, 128), 128), :]
    both = pick(end, placed(turning[0], range(4)))
    out_ref[:128, :] = both[:, :128]
    out_ref[128:256, :] = both[:, 128:256]
    out_ref[256:384, :] = dot(both[:, :256], both[:, 256:], NT)
    out_ref[384:, :] = half_ref[256:512, :]


def first_turns(place, half, start, end):
    return pl.pallas_call(
        first_kernel,
        out_shape=jax.ShapeDtypeStruct((640, 128), jnp.float32),
        in_specs=[SMEM, VMEM, VMEM, VMEM],
        out_specs=VMEM,
        scratch_shapes=TURNING,
        compiler_params=LIMIT,
    )(place, half, start, end)


def second_kernel(
    place_ref, own_ref, other_ref, start_ref, end_ref, whole_ref, out_ref, rms_ref,
    g_ref, held_rows, squares, in_sem, out_sems, *turning,
):
    fetch = pltpu.make_async_copy(whole_ref, held_rows, in_sem)
    fetch.start()
    core = place_ref[1]
    g_ref[core] = own_ref[...]
    g_ref[1 - core] = other_ref[...]
    basis = [jnp.concatenate([g_ref[i, :128, :], g_ref[i, 128:256, :]], axis=1) for i in range(2)]
    between = jnp.concatenate(
        [jnp.concatenate([g_ref[i, 384:512, :], g_ref[i, 512:640, :]], axis=1) for i in range(2)], axis=0
    )
    cross = dot(dot(basis[0], between), basis[1], NT)
    turn(square(g_ref[0, 256:384, :], cross, g_ref[1, 256:384, :]), start_ref[1], *turning)
    own_side = place_ref[0] // 2
    end = end_ref[1, pl.ds(pl.multiple_of(128 * own_side, 128), 128), :]
    last = pick(end, placed(turning[0], range(2)))
    turns = jnp.concatenate([dot(last[:, :128], basis[0]), dot(last[:, 128:], basis[1])], axis=1)
    diag = jnp.concatenate([turning[2][0], turning[2][1]], axis=0)
    sums = sum(short_dot(part[:, :8], end, (((0,), (1,)), ((), ()))) for part in reversed(split(diag, 3)))
    rms_ref[...] = jnp.sqrt(jnp.maximum(sums[:1], 0.0) / ROWS + EPS)
    turn_high, turn_low = split(turns, 2)
    both = jnp.concatenate([turn_high, turn_low], axis=0)
    fetch.wait()
    rows_each = held_rows.shape[1] // CHUNKS
    store = []
    for i in range(CHUNKS):
        rows = pl.ds(i * rows_each, rows_each)
        high, low = split(jnp.concatenate([held_rows[c, rows] for c in range(4)], axis=1), 2)
        wide = short_dot(high, both, NT)
        value = wide[:, :128] + (wide[:, 128:] + short_dot(low, turn_high, NT))
        squares[rows, :] = value * value
        store.append(pltpu.make_async_copy(squares.at[rows, :], out_ref.at[rows, :], out_sems.at[i]))
        store[-1].start()
    for copy in store:
        copy.wait()


def second_turns(place, own, other, start, end, whole):
    rows = whole.shape[1]
    return pl.pallas_call(
        second_kernel,
        out_shape=(
            jax.ShapeDtypeStruct((rows, 128), jnp.float32),
            jax.ShapeDtypeStruct((1, 128), jnp.float32),
        ),
        in_specs=[SMEM, VMEM, VMEM, VMEM, VMEM, HBM],
        out_specs=[HBM, VMEM],
        scratch_shapes=[
            pltpu.VMEM((2, 640, 128), jnp.float32),
            pltpu.VMEM((4, rows, 128), jnp.float32),
            pltpu.VMEM((rows, 128), jnp.float32),
            pltpu.SemaphoreType.DMA,
            pltpu.SemaphoreType.DMA((CHUNKS,)),
            *TURNING,
        ],
        compiler_params=pltpu.CompilerParams(vmem_limit_bytes=52 * 1024 * 1024),
    )(place, own, other, start, end, whole)


def places(order):
    return pl.pallas_call(
        places_kernel,
        out_shape=(jax.ShapeDtypeStruct((2, 256, 256), jnp.bfloat16),) * 2,
        in_specs=[VMEM],
        out_specs=[VMEM, VMEM],
        compiler_params=LIMIT,
    )(order)


def gram_kernel(core_ref, m_ref, mine_ref, theirs_ref):
    parts = [split(jnp.concatenate([m_ref[2 * a], m_ref[2 * a + 1]], axis=1), 2) for a in range(2)]

    def product(left, right):
        (lh, ll), (rh, rl) = left, right
        small = (short_dot(lh, rl, TN) + short_dot(ll, rh, TN)) + short_dot(ll, rl, TN)
        return short_dot(lh, rh, TN) + small

    low, high = slice(0, 128), slice(128, 256)
    between = product(*parts)
    row = lax.broadcasted_iota(jnp.int32, (128, 128), 0)
    col = lax.broadcasted_iota(jnp.int32, (128, 128), 1)
    halves = []
    for i, part in enumerate(parts):
        whole = product(part, part)
        own = (low, high)[i]
        diag = jnp.sum(jnp.where(row == col, whole[high, high], 0.0), axis=0, keepdims=True)
        packed = jnp.where(row <= col, whole[low, low], whole[high, high])
        blocks = [packed, whole[low, high], between[own, low], between[own, high]]
        rest = jnp.zeros((HALF_ROWS - 520, 128), jnp.float32)
        halves.append([*blocks, jnp.broadcast_to(diag, (8, 128)), rest])
    for core in range(2):

        @pl.when(core_ref[0] == core)
        def _(core=core):
            for ref, half in ((mine_ref, halves[core]), (theirs_ref, halves[1 - core])):
                at = 0
                for block in half:
                    ref[at : at + block.shape[0], :] = block
                    at += block.shape[0]


def grams(core_index, blocks):
    return pl.pallas_call(
        gram_kernel,
        out_shape=(jax.ShapeDtypeStruct((HALF_ROWS, 128), jnp.float32),) * 2,
        in_specs=[SMEM, VMEM],
        out_specs=[VMEM, VMEM],
        compiler_params=LIMIT,
    )(core_index, blocks)


def exchange(parts, axes):
    return lax.all_to_all(parts, axes, 0, 0, tiled=True)


def sum_part(value, axes):
    count = lax.axis_size(axes)
    return exchange(value.reshape(count, 1, value.size // count), axes).sum(0)


def collect(value, axes):
    return exchange(jnp.broadcast_to(value[None], (lax.axis_size(axes), *value.shape)), axes)


def swap_cores(value):
    return lax.ppermute(value, "core", ((0, 1), (1, 0)))


def local(matrix, order):
    place = jnp.stack([lax.axis_index("x"), lax.axis_index("core")]).astype(jnp.int32)
    blocks = exchange(matrix.reshape(4, 512, 128), "x")
    matrix, blocks = lax.optimization_barrier((matrix, blocks))
    whole = lax.all_gather(matrix, "x")
    mine, theirs = grams(place[1:], blocks)
    theirs, place, start, end = lax.optimization_barrier((swap_cores(theirs), place, *places(order)))
    gram = mine + theirs
    gram = collect(sum_part(gram, ("y", "x")), "z").sum(0)
    half = collect(gram, ("y", "x")).reshape(HALF_ROWS, 128)
    own = first_turns(place, half, start, end)
    density, rms = second_turns(place, own, swap_cores(own), start, end, whole)
    return density, rms.reshape(128)


def solution(mesh):
    fine = Mesh(mesh.devices.reshape(8, 8, 2, 4), ("z", "y", "core", "x"))
    rows = ("z", "y", "core")
    return jax.shard_map(
        local,
        mesh=fine,
        in_specs=(P(rows, "x"), P()),
        out_specs=(P(rows, "x"), P("x")),
        check_vma=False,
    )
```

time: 113 us -> 110 us (0.973)
  Pallas kernels: 15.2 us -> 12.4 us
    pallas_call x1 -> x2, Pallas kernels: 13.7 us -> 10.9 us  [the longest x1 7.07 us: second_turns(): pl.pallas_call(second_kernel, out_shape=(jax.ShapeDtypeStruct((rows, 128)...]
  transfers between devices with their start and end apart: 3 -> 3, of which waited for: 2 -> 2; matrix products, arithmetic and copies ran while one was open for 0% -> 0% of each run, Pallas kernels for 1% -> 5%
where the time goes in v7:
time: 110 us; the launch traced here: 109 us
  blocking collectives  66 us (60%)
  starting transfers between devices  14.6 us (13%)
  between operations  14.1 us (13%)
  Pallas kernels  12.4 us (11%)
  waiting for transfers between devices  1.93 us (2%)
    all_to_all x4, blocking collectives, exchange(): return lax.all_to_all(parts, axes, 0, 0, tiled=True)  66 us
    ppermute x2, starting transfers between devices, swap_cores(): return lax.ppermute(value, 'core', ((0, 1), (1, 0)))  14.6 us
    pallas_call x1, Pallas kernels, second_turns(): pl.pallas_call(second_kernel, out_shape=(jax.ShapeDtypeStruct((rows, 128)...  7.07 us
    pallas_call x1, Pallas kernels, first_turns(): pl.pallas_call(first_kernel, out_shape=jax.ShapeDtypeStruct((640, 128), j...  3.83 us
  transfers between devices with their start and end apart: 3, of which 2 were waited for; matrix products, arithmetic and copies ran while one was open for 0% of the time, Pallas kernels for 5%

profile of v7, /device:TPU:1, one launch (start us, length us, event | category | flops | bytes accessed | tf_op | source)
XLA Modules:
  0.0 109.5 jit_solution(10267790994434609811)
XLA Ops:
  7.2 0.0 copy-start
  7.2 0.0 all-gather.3.cloned.1.call-start
  7.2 14.6 %all_to_all.20.m_ref = f32[4,512,128]{2,1,0:T(8,128)S(1)} all-to-all(f32[4,512,128]{2,1,0:T(8,128)} %bitcast.9), channel_id=1, replica_groups=mesh['z'=8,'y'=8,'core'=2,'x'=4] {'x'}, dimensions={0} | all-to-all | bytes 2097152 | tf_op jit(solution)/shard_map/all_to_all | solution.py:296
  21.8 0.0 all-gather.3.cloned.1.call-update
  21.8 1.1 shard_map.41
  22.9 8.6 %collective-permute-start = (f32[544,128]{1,0:T(8,128)S(1)}, f32[544,128]{1,0:T(8,128)S(1)}, u32[]{:S(2)}, u32[]{:S(2)}) collective-permute-start(f32[544,128]{1,0:T(8,128)S(1)} %get-tuple-element.15), channel_id=1, source_target_pairs={{0,4},{4,0},{1,5},{5,1},{2,6},{6,2},{3,7},{7,3},{8,12},{12,8},{9,1... | collective-permute-start | bytes 835592 | tf_op jit(solution)/shard_map/ppermute | solution.py:309
  31.5 0.0 copy-done
  31.5 0.4 shard_map.42
  31.9 0.1 pad_add_fusion.place_ref
  32.0 0.7 collective-permute-done
  32.7 19.3 %all_to_all.21 = f32[32,1,2176]{2,1,0:T(1,128)S(1)} all-to-all(f32[32,1,2176]{2,1,0:T(1,128)S(1)} %bitcast.10), channel_id=1, replica_groups=mesh['z'=8,'y'=8,'core'=2,'x'=4] {'y','x'}, dimensions={0} | all-to-all | bytes 557056 | tf_op jit(solution)/shard_map/all_to_all | solution.py:296
  52.0 0.2 reduce_sum.18
  52.2 17.1 %all_to_all.22 = f32[8,1,2176]{2,1,0:T(1,128)S(1)} all-to-all(f32[8,1,2176]{2,1,0:T(1,128)S(1)} %broadcast_in_dim.4), channel_id=1, replica_groups=mesh['z'=8,'y'=8,'core'=2,'x'=4] {'z'}, dimensions={0} | all-to-all | bytes 139264 | tf_op jit(solution)/shard_map/all_to_all | solution.py:296
  69.3 0.1 reduce_sum.19
  69.3 0.1 broadcast_in_dim.5
  69.5 15.0 %all_to_all.23 = f32[32,1,2176]{2,1,0:T(1,128)S(1)} all-to-all(f32[32,1,2176]{2,1,0:T(1,128)S(1)} %broadcast_in_dim.5), channel_id=1, replica_groups=mesh['z'=8,'y'=8,'core'=2,'x'=4] {'y','x'}, dimensions={0} | all-to-all | bytes 557056 | tf_op jit(solution)/shard_map/all_to_all | solution.py:296
  84.5 3.8 %shard_map.43.own_ref = f32[640,128]{1,0:T(8,128)S(1)} custom-call(s32[2]{0:T(128)S(1)} %pad_add_fusion.place_ref, f32[544,128]{1,0:T(8,128)S(1)} %bitcast.7, bf16[2,256,256]{2,1,0:T(8,128)(2,1)S(1)} %get-tuple-element.21.start_ref, bf16[2,256,256]{2,1,0:T(8,128)(2,1)S(1)} %get-tuple-element.22.end_ref), custom_call_target="tpu_custom_call" | custom-call | tf_op jit(solution)/shard_map/pallas_call | solution.py:172
  88.3 6.0 %collective-permute-start.1 = (f32[640,128]{1,0:T(8,128)S(1)}, f32[640,128]{1,0:T(8,128)S(1)}, u32[]{:S(2)}, u32[]{:S(2)}) collective-permute-start(f32[640,128]{1,0:T(8,128)S(1)} %shard_map.43.own_ref), channel_id=1, source_target_pairs={{0,4},{4,0},{1,5},{5,1},{2,6},{6,2},{3,7},{7,3},{8,12},{12,8},{9,1... | collective-permute-start | bytes 983048 | tf_op jit(solution)/shard_map/ppermute | solution.py:309
  94.3 1.2 %collective-permute-done.1.other_ref = f32[640,128]{1,0:T(8,128)S(1)} collective-permute-done((f32[640,128]{1,0:T(8,128)S(1)}, f32[640,128]{1,0:T(8,128)S(1)}, u32[]{:S(2)}, u32[]{:S(2)}) %collective-permute-start.1) | collective-permute-done | bytes 327712 | tf_op jit(solution)/shard_map/ppermute | solution.py:309
  95.6 0.0 all-gather.3.cloned.1.call-done
  95.6 7.1 %shard_map.44 = (f32[2048,128]{1,0:T(8,128)}, f32[1,128]{1,0:T(1,128)}) custom-call(s32[2]{0:T(128)S(1)} %pad_add_fusion.place_ref, f32[640,128]{1,0:T(8,128)S(1)} %shard_map.43.own_ref, f32[640,128]{1,0:T(8,128)S(1)} %collective-permute-done.1.other_ref, bf16[2,256,256]{2,1,0:T(8,128)(2,1)S(1)} %get-tuple-element.21.start_ref, ...), custom_call_target="tpu_custom_call" | custom-call | tf_op jit(solution)/shard_map/pallas_call | solution.py:223
  (2 shorter events, 0.1 us)
Async XLA Ops:
  7.2 24.3 %copy-start = (s32[2,256]{1,0:T(2,128)S(1)}, s32[2,256]{1,0:T(2,128)}, u32[]{:S(2)}) copy-start(s32[2,256]{1,0:T(2,128)} %order_ref.1) | copy-start | bytes 6148
  7.2 88.4 %all-gather.3.cloned.1.call-start = ((), (), s32[]{:S(2)}) async-start(), calls=%async_computation.4 | async-start | bytes 5242880 | tf_op jit(solution)/shard_map/all_gather | solution.py:316
  22.9 9.7 %collective-permute-start = (f32[544,128]{1,0:T(8,128)S(1)}, f32[544,128]{1,0:T(8,128)S(1)}, u32[]{:S(2)}, u32[]{:S(2)}) collective-permute-start(f32[544,128]{1,0:T(8,128)S(1)} %get-tuple-element.15), channel_id=1, source_target_pairs={{0,4},{4,0},{1,5},{5,1},{2,6},{6,2},{3,7},{7,3},{8,12},{12,8},{9,1... | collective-permute-start | bytes 835592 | tf_op jit(solution)/shard_map/ppermute | solution.py:309
  88.3 7.2 %collective-permute-start.1 = (f32[640,128]{1,0:T(8,128)S(1)}, f32[640,128]{1,0:T(8,128)S(1)}, u32[]{:S(2)}, u32[]{:S(2)}) collective-permute-start(f32[640,128]{1,0:T(8,128)S(1)} %shard_map.43.own_ref), channel_id=1, source_target_pairs={{0,4},{4,0},{1,5},{5,1},{2,6},{6,2},{3,7},{7,3},{8,12},{12,8},{9,1... | collective-permute-start | bytes 983048 | tf_op jit(solution)/shard_map/ppermute | solution.py:309
Sparse Core Ops, SparseCore 0:
  22.0 65.6 all-gather.2

commit v8 on v7

--- a/solution.py
+++ b/solution.py
@@ -17,7 +17,7 @@
 VMEM = pl.BlockSpec(memory_space=pltpu.VMEM)
 SMEM = pl.BlockSpec(memory_space=pltpu.SMEM)
 HBM = pl.BlockSpec(memory_space=pltpu.HBM)
-CHUNKS = 4
+QUARTER = 512
 
 
 def dot(a, b, dims=NN):
@@ -180,11 +180,15 @@
 
 
 def second_kernel(
-    place_ref, own_ref, other_ref, start_ref, end_ref, whole_ref, out_ref, rms_ref,
-    g_ref, held_rows, squares, in_sem, out_sems, *turning,
+    place_ref, own_ref, other_ref, start_ref, end_ref, blocks_ref, matrix_ref, ref1, ref2, ref3, out_ref, rms_ref,
+    g_ref, q_ref, matrix_rows, held_rows, squares, in_sems, out_sems, *turning,
 ):
-    fetch = pltpu.make_async_copy(whole_ref, held_rows, in_sem)
-    fetch.start()
+    x = place_ref[0]
+    fetch = [pltpu.make_async_copy(matrix_ref, matrix_rows, in_sems.at[0])]
+    for i, ref in enumerate((ref1, ref2, ref3)):
+        fetch.append(pltpu.make_async_copy(ref, held_rows.at[i], in_sems.at[i + 1]))
+    for copy in fetch:
+        copy.start()
     core = place_ref[1]
     g_ref[core] = own_ref[...]
     g_ref[1 - core] = other_ref[...]
@@ -198,46 +202,83 @@
     end = end_ref[1, pl.ds(pl.multiple_of(128 * own_side, 128), 128), :]
     last = pick(end, placed(turning[0], range(2)))
     turns = jnp.concatenate([dot(last[:, :128], basis[0]), dot(last[:, 128:], basis[1])], axis=1)
+    turn_high, turn_low = split(turns, 2)
+    for block in range(4):
+        cols = slice(128 * block, 128 * block + 128)
+        q_ref[block] = jnp.concatenate([turn_high[:, cols], turn_low[:, cols]], axis=0)
+    both = jnp.concatenate([q_ref[lax.rem(place_ref[0] + i, 4)] for i in range(4)], axis=1)
+    turn_high = both[:128]
+    for copy in fetch:
+        copy.wait()
+    store = []
+    for j in range(4):
+        rows = pl.ds(pl.multiple_of(QUARTER * lax.rem(x + j, 4), QUARTER), QUARTER)
+        parts = [matrix_rows[rows, :]]
+        for i in range(1, 4):
+            if j == 0:
+                parts.append(blocks_ref[lax.rem(x + i, 4)])
+            else:
+                parts.append(held_rows[i - 1, QUARTER * (j - 1) : QUARTER * j, :])
+        high, low = split(jnp.concatenate(parts, axis=1), 2)
+        wide = short_dot(high, both, NT)
+        value = wide[:, :128] + (wide[:, 128:] + short_dot(low, turn_high, NT))
+        squares[j] = value * value
+        store.append(pltpu.make_async_copy(squares.at[j], out_ref.at[rows, :], out_sems.at[j]))
+        store[-1].start()
     diag = jnp.concatenate([turning[2][0], turning[2][1]], axis=0)
     sums = sum(short_dot(part[:, :8], end, (((0,), (1,)), ((), ()))) for part in reversed(split(diag, 3)))
     rms_ref[...] = jnp.sqrt(jnp.maximum(sums[:1], 0.0) / ROWS + EPS)
-    turn_high, turn_low = split(turns, 2)
-    both = jnp.concatenate([turn_high, turn_low], axis=0)
-    fetch.wait()
-    rows_each = held_rows.shape[1] // CHUNKS
-    store = []
-    for i in range(CHUNKS):
-        rows = pl.ds(i * rows_each, rows_each)
-        high, low = split(jnp.concatenate([held_rows[c, rows] for c in range(4)], axis=1), 2)
-        wide = short_dot(high, both, NT)
-        value = wide[:, :128] + (wide[:, 128:] + short_dot(low, turn_high, NT))
-        squares[rows, :] = value * value
-        store.append(pltpu.make_async_copy(squares.at[rows, :], out_ref.at[rows, :], out_sems.at[i]))
-        store[-1].start()
     for copy in store:
         copy.wait()
 
 
-def second_turns(place, own, other, start, end, whole):
-    rows = whole.shape[1]
+def second_turns(place, own, other, start, end, blocks, matrix, *others):
+    rows = matrix.shape[0]
     return pl.pallas_call(
         second_kernel,
         out_shape=(
             jax.ShapeDtypeStruct((rows, 128), jnp.float32),
             jax.ShapeDtypeStruct((1, 128), jnp.float32),
         ),
-        in_specs=[SMEM, VMEM, VMEM, VMEM, VMEM, HBM],
+        in_specs=[SMEM, VMEM, VMEM, VMEM, VMEM, VMEM, HBM, HBM, HBM, HBM],
         out_specs=[HBM, VMEM],
         scratch_shapes=[
             pltpu.VMEM((2, 640, 128), jnp.float32),
-            pltpu.VMEM((4, rows, 128), jnp.float32),
+            pltpu.VMEM((4, 256, 128), jnp.bfloat16),
             pltpu.VMEM((rows, 128), jnp.float32),
-            pltpu.SemaphoreType.DMA,
-            pltpu.SemaphoreType.DMA((CHUNKS,)),
+            pltpu.VMEM((3, 3 * QUARTER, 128), jnp.float32),
+            pltpu.VMEM((4, QUARTER, 128), jnp.float32),
+            pltpu.SemaphoreType.DMA((4,)),
+            pltpu.SemaphoreType.DMA((4,)),
             *TURNING,
         ],
         compiler_params=pltpu.CompilerParams(vmem_limit_bytes=52 * 1024 * 1024),
-    )(place, own, other, start, end, whole)
+    )(place, own, other, start, end, blocks, matrix, *others)
+
+
+def other_quarters_kernel(place_ref, m_ref, *refs):
+    outs, sems = refs[:3], refs[3]
+    copies = []
+    for i, out in enumerate(outs):
+        for j in range(3):
+            quarter = lax.rem(place_ref[0] + 4 - i + j, 4)
+            rows = pl.ds(pl.multiple_of(QUARTER * quarter, QUARTER), QUARTER)
+            copies.append(pltpu.make_async_copy(m_ref.at[rows, :], out.at[pl.ds(QUARTER * j, QUARTER), :], sems.at[i, j]))
+    for copy in copies:
+        copy.start()
+    for copy in copies:
+        copy.wait()
+
+
+def other_quarters(place, matrix):
+    return pl.pallas_call(
+        other_quarters_kernel,
+        out_shape=(jax.ShapeDtypeStruct((3 * QUARTER, 128), jnp.float32),) * 3,
+        in_specs=[SMEM, HBM],
+        out_specs=[HBM] * 3,
+        scratch_shapes=[pltpu.SemaphoreType.DMA((3, 3))],
+        compiler_params=LIMIT,
+    )(place, matrix)
 
 
 def places(order):
@@ -309,18 +350,25 @@
     return lax.ppermute(value, "core", ((0, 1), (1, 0)))
 
 
+def from_next(value, distance):
+    return lax.ppermute(value, "x", [((i + distance) % 4, i) for i in range(4)])
+
+
 def local(matrix, order):
     place = jnp.stack([lax.axis_index("x"), lax.axis_index("core")]).astype(jnp.int32)
-    blocks = exchange(matrix.reshape(4, 512, 128), "x")
-    matrix, blocks = lax.optimization_barrier((matrix, blocks))
-    whole = lax.all_gather(matrix, "x")
+    parts = other_quarters(place, matrix)
+    blocks = exchange(matrix.reshape(4, QUARTER, 128), "x")
+    blocks, *parts = lax.optimization_barrier((blocks, *parts))
     mine, theirs = grams(place[1:], blocks)
     theirs, place, start, end = lax.optimization_barrier((swap_cores(theirs), place, *places(order)))
-    gram = mine + theirs
-    gram = collect(sum_part(gram, ("y", "x")), "z").sum(0)
+    gram, *parts = lax.optimization_barrier((mine + theirs, *parts))
+    others = [from_next(part, i + 1) for i, part in enumerate(parts)]
+    gram = sum_part(gram, ("y", "x"))
+    gram = collect(gram, "z").sum(0)
     half = collect(gram, ("y", "x")).reshape(HALF_ROWS, 128)
+    half, *others = lax.optimization_barrier((half, *others))
     own = first_turns(place, half, start, end)
-    density, rms = second_turns(place, own, swap_cores(own), start, end, whole)
+    density, rms = second_turns(place, own, swap_cores(own), start, end, blocks, matrix, *others)
     return density, rms.reshape(128)
 
 

time: 110 us -> 101 us (0.918)
  blocking collectives: 66 us -> 17.1 us
  starting transfers between devices: 14.6 us -> 42.7 us
  waiting for transfers between devices: 1.93 us -> 22.3 us
  between operations: 14.1 us -> 0.79 us
  local copies, waits for them, and re-layouts: 0.19 us -> 2.74 us
  Pallas kernels: 12.4 us -> 13.9 us
    all_to_all x4 -> x1, blocking collectives: 66 us -> 17.1 us  [exchange(): return lax.all_to_all(parts, axes, 0, 0, tiled=True)]
    all_to_all x0 -> x3, starting transfers between devices: none -> 18.3 us  [exchange(): return lax.all_to_all(parts, axes, 0, 0, tiled=True)]
    all_to_all x0 -> x3, waiting for transfers between devices: none -> 10.3 us  [exchange(): return lax.all_to_all(parts, axes, 0, 0, tiled=True)]
    ppermute x0 -> x3, waiting for transfers between devices: none -> 9.92 us  [from_next(): return lax.ppermute(value, 'x', [((i + distance) % 4, i) for i in range(4)])]
    ppermute x0 -> x3, starting transfers between devices: none -> 9.32 us  [from_next(): return lax.ppermute(value, 'x', [((i + distance) % 4, i) for i in range(4)])]
    unnamed x2 -> x12, local copies, waits for them, and re-layouts: 0.01 us -> 1.83 us
  transfers between devices with their start and end apart: 3 -> 8, of which waited for: 2 -> 6; matrix products, arithmetic and copies ran while one was open for 0% -> 1% of each run, Pallas kernels for 5% -> 1%
where the time goes in v8:
time: 101 us
  starting transfers between devices  42.7 us (42%)
  waiting for transfers between devices  22.3 us (22%)
  blocking collectives  17.1 us (17%)
  Pallas kernels  13.9 us (14%)
  local copies, waits for them, and re-layouts  2.74 us (3%)
  other arithmetic  1.08 us (1%)
    all_to_all x3, starting transfers between devices, exchange(): return lax.all_to_all(parts, axes, 0, 0, tiled=True)  18.3 us
    all_to_all x1, blocking collectives, exchange(): return lax.all_to_all(parts, axes, 0, 0, tiled=True)  17.1 us
    ppermute x2, starting transfers between devices, swap_cores(): return lax.ppermute(value, 'core', ((0, 1), (1, 0)))  15.1 us
    all_to_all x3, waiting for transfers between devices, exchange(): return lax.all_to_all(parts, axes, 0, 0, tiled=True)  10.3 us
    ppermute x3, waiting for transfers between devices, from_next(): return lax.ppermute(value, 'x', [((i + distance) % 4, i) for i in range(4)])  9.92 us
    ppermute x3, starting transfers between devices, from_next(): return lax.ppermute(value, 'x', [((i + distance) % 4, i) for i in range(4)])  9.32 us
    pallas_call x1, Pallas kernels, second_turns(): pl.pallas_call(second_kernel, out_shape=(jax.ShapeDtypeStruct((rows, 128)...  7.81 us
    pallas_call x1, Pallas kernels, first_turns(): pl.pallas_call(first_kernel, out_shape=jax.ShapeDtypeStruct((640, 128), j...  3.83 us
  transfers between devices with their start and end apart: 8, of which 6 were waited for; matrix products, arithmetic and copies ran while one was open for 1% of the time, Pallas kernels for 1%

profile of v8, /device:TPU:1, one launch (start us, length us, event | category | flops | bytes accessed | tf_op | source)
XLA Modules:
  0.0 100.6 jit_solution(6696679759964401395)
XLA Ops:
  0.6 5.0 %all-to-all-start = ((f32[4,512,128]{2,1,0:T(8,128)}), f32[4,512,128]{2,1,0:T(8,128)S(1)}, u32[]{:S(2)}, u32[]{:S(2)}) async-start(f32[4,512,128]{2,1,0:T(8,128)} %bitcast.6), calls=%async_computation | async-start | bytes 2097152 | tf_op jit(solution)/shard_map/all_to_all | solution.py:337
  5.7 0.8 shard_map.41
  6.5 0.9 copy-done.3
  7.5 0.9 copy-done.5
  8.3 7.0 %all-to-all-done.m_ref.blocks_ref = f32[4,512,128]{2,1,0:T(8,128)S(1)} async-done(((f32[4,512,128]{2,1,0:T(8,128)}), f32[4,512,128]{2,1,0:T(8,128)S(1)}, u32[]{:S(2)}, u32[]{:S(2)}) %all-to-all-start) | async-done | bytes 1048608 | tf_op jit(solution)/shard_map/all_to_all | solution.py:337
  15.4 1.1 %shard_map.42 = (f32[544,128]{1,0:T(8,128)S(1)}, f32[544,128]{1,0:T(8,128)S(1)}) custom-call(s32[1]{0:T(128)} %bitcast.core_ref, f32[4,512,128]{2,1,0:T(8,128)S(1)} %all-to-all-done.m_ref.blocks_ref), custom_call_target="tpu_custom_call" | custom-call | tf_op jit(solution)/shard_map/pallas_call | solution.py:327
  16.4 8.7 %collective-permute-start = (f32[544,128]{1,0:T(8,128)S(1)}, f32[544,128]{1,0:T(8,128)S(1)}, u32[]{:S(2)}, u32[]{:S(2)}) collective-permute-start(f32[544,128]{1,0:T(8,128)S(1)} %get-tuple-element.31), channel_id=1, source_target_pairs={{0,4},{4,0},{1,5},{5,1},{2,6},{6,2},{3,7},{7,3},{8,12},{12,8},{9,1... | collective-permute-start | bytes 835592 | tf_op jit(solution)/shard_map/ppermute | solution.py:350
  25.2 0.4 shard_map.43
  25.6 0.8 collective-permute-done
  26.3 0.8 add.3
  27.1 7.5 %all-to-all-start.1 = ((f32[32,1,2176]{2,1,0:T(1,128)}), f32[32,1,2176]{2,1,0:T(1,128)S(1)}, u32[]{:S(2)}, u32[]{:S(2)}) async-start(f32[32,1,2176]{2,1,0:T(1,128)} %bitcast.8), calls=%async_computation.1 | async-start | bytes 557056 | tf_op jit(solution)/shard_map/all_to_all | solution.py:337
  34.6 4.3 %collective-permute-start.1 = (f32[1536,128]{1,0:T(8,128)}, f32[1536,128]{1,0:T(8,128)S(1)}, u32[]{:S(2)}, u32[]{:S(2)}) collective-permute-start(f32[1536,128]{1,0:T(8,128)} %copy-done.5), channel_id=1, source_target_pairs={{1,0},{2,1},{3,2},{0,3},{5,4},{6,5},{7,6},{4,7},{9,8},{10,9},{11,1... | collective-permute-start | bytes 2359304 | tf_op jit(solution)/shard_map/ppermute | solution.py:354
  38.9 2.5 %collective-permute-start.2 = (f32[1536,128]{1,0:T(8,128)S(1)}, f32[1536,128]{1,0:T(8,128)}, u32[]{:S(2)}, u32[]{:S(2)}) collective-permute-start(f32[1536,128]{1,0:T(8,128)S(1)} %copy-done.4), channel_id=1, source_target_pairs={{2,0},{3,1},{0,2},{1,3},{6,4},{7,5},{4,6},{5,7},{10,8},{11,9},{8,1... | collective-permute-start | bytes 2359304 | tf_op jit(solution)/shard_map/ppermute | solution.py:354
  41.4 2.5 %collective-permute-start.3 = (f32[1536,128]{1,0:T(8,128)S(1)}, f32[1536,128]{1,0:T(8,128)}, u32[]{:S(2)}, u32[]{:S(2)}) collective-permute-start(f32[1536,128]{1,0:T(8,128)S(1)} %get-tuple-element.43), channel_id=1, source_target_pairs={{3,0},{0,1},{1,2},{2,3},{7,4},{4,5},{5,6},{6,7},{11,8},{8,9},{9,10... | collective-permute-start | bytes 2359304 | tf_op jit(solution)/shard_map/ppermute | solution.py:354
  43.9 2.7 %all-to-all-done.1 = f32[32,1,2176]{2,1,0:T(1,128)S(1)} async-done(((f32[32,1,2176]{2,1,0:T(1,128)}), f32[32,1,2176]{2,1,0:T(1,128)S(1)}, u32[]{:S(2)}, u32[]{:S(2)}) %all-to-all-start.1) | async-done | bytes 278560 | tf_op jit(solution)/shard_map/all_to_all | solution.py:337
  46.9 17.1 %all_to_all.20 = f32[8,1,2176]{2,1,0:T(1,128)S(1)} all-to-all(f32[8,1,2176]{2,1,0:T(1,128)S(1)} %broadcast_in_dim.4), channel_id=1, replica_groups=mesh['z'=8,'y'=8,'core'=2,'x'=4] {'z'}, dimensions={0} | all-to-all | bytes 139264 | tf_op jit(solution)/shard_map/all_to_all | solution.py:337
  64.0 0.9 broadcast_in_dim.5
  64.9 5.9 %all-to-all-start.3 = ((f32[32,1,2176]{2,1,0:T(1,128)}), f32[32,1,2176]{2,1,0:T(1,128)S(1)}, u32[]{:S(2)}, u32[]{:S(2)}) async-start(f32[32,1,2176]{2,1,0:T(1,128)} %broadcast_in_dim.5), calls=%async_computation.3 | async-start | bytes 557056 | tf_op jit(solution)/shard_map/all_to_all | solution.py:337
  70.8 9.9 %collective-permute-done.3.ref3 = f32[1536,128]{1,0:T(8,128)} collective-permute-done((f32[1536,128]{1,0:T(8,128)S(1)}, f32[1536,128]{1,0:T(8,128)}, u32[]{:S(2)}, u32[]{:S(2)}) %collective-permute-start.3) | collective-permute-done | bytes 786464 | tf_op jit(solution)/shard_map/ppermute | solution.py:354
  80.7 0.6 all-to-all-done.3
  81.3 3.8 %shard_map.44.own_ref = f32[640,128]{1,0:T(8,128)S(1)} custom-call(s32[2]{0:T(128)S(1)} %pad_add_fusion.place_ref, f32[544,128]{1,0:T(8,128)S(1)} %bitcast.7, bf16[2,256,256]{2,1,0:T(8,128)(2,1)S(1)} %get-tuple-element.45.start_ref, bf16[2,256,256]{2,1,0:T(8,128)(2,1)S(1)} %get-tuple-element.46.end_ref), custom_call_target="tpu_custom_call" | custom-call | tf_op jit(solution)/shard_map/pallas_call | solution.py:172
  85.2 6.4 %collective-permute-start.4 = (f32[640,128]{1,0:T(8,128)S(1)}, f32[640,128]{1,0:T(8,128)S(1)}, u32[]{:S(2)}, u32[]{:S(2)}) collective-permute-start(f32[640,128]{1,0:T(8,128)S(1)} %shard_map.44.own_ref), channel_id=1, source_target_pairs={{0,4},{4,0},{1,5},{5,1},{2,6},{6,2},{3,7},{7,3},{8,12},{12,8},{9,1... | collective-permute-start | bytes 983048 | tf_op jit(solution)/shard_map/ppermute | solution.py:350
  91.5 1.2 %collective-permute-done.4.other_ref = f32[640,128]{1,0:T(8,128)S(1)} collective-permute-done((f32[640,128]{1,0:T(8,128)S(1)}, f32[640,128]{1,0:T(8,128)S(1)}, u32[]{:S(2)}, u32[]{:S(2)}) %collective-permute-start.4) | collective-permute-done | bytes 327712 | tf_op jit(solution)/shard_map/ppermute | solution.py:350
  92.8 7.8 %shard_map.45 = (f32[2048,128]{1,0:T(8,128)}, f32[1,128]{1,0:T(1,128)}) custom-call(s32[2]{0:T(128)S(1)} %pad_add_fusion.place_ref, f32[640,128]{1,0:T(8,128)S(1)} %shard_map.44.own_ref, f32[640,128]{1,0:T(8,128)S(1)} %collective-permute-done.4.other_ref, bf16[2,256,256]{2,1,0:T(8,128)(2,1)S(1)} %get-tuple-element.45.start_ref, ...), custom_call_target="tpu_custom_call" | custom-call | tf_op jit(solution)/shard_map/pallas_call | solution.py:237
  (16 shorter events, 0.4 us)
Async XLA Ops:
  0.6 5.1 %copy-start = (f32[2048,128]{1,0:T(8,128)S(1)}, f32[2048,128]{1,0:T(8,128)}, u32[]{:S(2)}) copy-start(f32[2048,128]{1,0:T(8,128)} %matrix_ref.1) | copy-start | bytes 3145732
  0.6 14.7 %all-to-all-start = ((f32[4,512,128]{2,1,0:T(8,128)}), f32[4,512,128]{2,1,0:T(8,128)S(1)}, u32[]{:S(2)}, u32[]{:S(2)}) async-start(f32[4,512,128]{2,1,0:T(8,128)} %bitcast.6), calls=%async_computation | async-start | bytes 2097152 | tf_op jit(solution)/shard_map/all_to_all | solution.py:337
  6.5 0.9 copy-start.3
  7.5 0.9 copy-start.5
  15.4 11.7 %copy-start.1 = (f32[4,512,128]{2,1,0:T(8,128)}, f32[4,512,128]{2,1,0:T(8,128)S(1)}, u32[]{:S(2)}) copy-start(f32[4,512,128]{2,1,0:T(8,128)S(1)} %all-to-all-done.m_ref.blocks_ref) | copy-start | bytes 3145732
  15.4 9.8 %copy-start.2 = (s32[2,256]{1,0:T(2,128)S(1)}, s32[2,256]{1,0:T(2,128)}, u32[]{:S(2)}) copy-start(s32[2,256]{1,0:T(2,128)} %order_ref.1) | copy-start | bytes 6148
  16.4 22.5 %copy-start.4 = (f32[1536,128]{1,0:T(8,128)S(1)}, f32[1536,128]{1,0:T(8,128)}, u32[]{:S(2)}) copy-start(f32[1536,128]{1,0:T(8,128)} %copy-done.3) | copy-start | bytes 2359300
  16.4 9.9 %collective-permute-start = (f32[544,128]{1,0:T(8,128)S(1)}, f32[544,128]{1,0:T(8,128)S(1)}, u32[]{:S(2)}, u32[]{:S(2)}) collective-permute-start(f32[544,128]{1,0:T(8,128)S(1)} %get-tuple-element.31), channel_id=1, source_target_pairs={{0,4},{4,0},{1,5},{5,1},{2,6},{6,2},{3,7},{7,3},{8,12},{12,8},{9,1... | collective-permute-start | bytes 835592 | tf_op jit(solution)/shard_map/ppermute | solution.py:350
  27.1 19.5 %all-to-all-start.1 = ((f32[32,1,2176]{2,1,0:T(1,128)}), f32[32,1,2176]{2,1,0:T(1,128)S(1)}, u32[]{:S(2)}, u32[]{:S(2)}) async-start(f32[32,1,2176]{2,1,0:T(1,128)} %bitcast.8), calls=%async_computation.1 | async-start | bytes 557056 | tf_op jit(solution)/shard_map/all_to_all | solution.py:337
  34.6 36.2 %collective-permute-start.1 = (f32[1536,128]{1,0:T(8,128)}, f32[1536,128]{1,0:T(8,128)S(1)}, u32[]{:S(2)}, u32[]{:S(2)}) collective-permute-start(f32[1536,128]{1,0:T(8,128)} %copy-done.5), channel_id=1, source_target_pairs={{1,0},{2,1},{3,2},{0,3},{5,4},{6,5},{7,6},{4,7},{9,8},{10,9},{11,1... | collective-permute-start | bytes 2359304 | tf_op jit(solution)/shard_map/ppermute | solution.py:354
  38.9 31.9 %collective-permute-start.2 = (f32[1536,128]{1,0:T(8,128)S(1)}, f32[1536,128]{1,0:T(8,128)}, u32[]{:S(2)}, u32[]{:S(2)}) collective-permute-start(f32[1536,128]{1,0:T(8,128)S(1)} %copy-done.4), channel_id=1, source_target_pairs={{2,0},{3,1},{0,2},{1,3},{6,4},{7,5},{4,6},{5,7},{10,8},{11,9},{8,1... | collective-permute-start | bytes 2359304 | tf_op jit(solution)/shard_map/ppermute | solution.py:354
  41.4 39.3 %collective-permute-start.3 = (f32[1536,128]{1,0:T(8,128)S(1)}, f32[1536,128]{1,0:T(8,128)}, u32[]{:S(2)}, u32[]{:S(2)}) collective-permute-start(f32[1536,128]{1,0:T(8,128)S(1)} %get-tuple-element.43), channel_id=1, source_target_pairs={{3,0},{0,1},{1,2},{2,3},{7,4},{4,5},{5,6},{6,7},{11,8},{8,9},{9,10... | collective-permute-start | bytes 2359304 | tf_op jit(solution)/shard_map/ppermute | solution.py:354
  64.9 16.4 %all-to-all-start.3 = ((f32[32,1,2176]{2,1,0:T(1,128)}), f32[32,1,2176]{2,1,0:T(1,128)S(1)}, u32[]{:S(2)}, u32[]{:S(2)}) async-start(f32[32,1,2176]{2,1,0:T(1,128)} %broadcast_in_dim.5), calls=%async_computation.3 | async-start | bytes 557056 | tf_op jit(solution)/shard_map/all_to_all | solution.py:337
  85.2 7.6 %collective-permute-start.4 = (f32[640,128]{1,0:T(8,128)S(1)}, f32[640,128]{1,0:T(8,128)S(1)}, u32[]{:S(2)}, u32[]{:S(2)}) collective-permute-start(f32[640,128]{1,0:T(8,128)S(1)} %shard_map.44.own_ref), channel_id=1, source_target_pairs={{0,4},{4,0},{1,5},{5,1},{2,6},{6,2},{3,7},{7,3},{8,12},{12,8},{9,1... | collective-permute-start | bytes 983048 | tf_op jit(solution)/shard_map/ppermute | solution.py:350

commit v9 on v8

--- a/solution.py
+++ b/solution.py
@@ -366,8 +366,8 @@
     gram = sum_part(gram, ("y", "x"))
     gram = collect(gram, "z").sum(0)
     half = collect(gram, ("y", "x")).reshape(HALF_ROWS, 128)
-    half, *others = lax.optimization_barrier((half, *others))
     own = first_turns(place, half, start, end)
+    own, *others = lax.optimization_barrier((own, *others))
     density, rms = second_turns(place, own, swap_cores(own), start, end, blocks, matrix, *others)
     return density, rms.reshape(128)
 

time: 101 us -> 100 us (0.990)
  blocking collectives: 17.1 us -> 34.5 us
  waiting for transfers between devices: 22.3 us -> 11.7 us
  starting transfers between devices: 42.7 us -> 35.6 us
    all_to_all x1 -> x2, blocking collectives: 17.1 us -> 34.5 us  [exchange(): return lax.all_to_all(parts, axes, 0, 0, tiled=True)]
    ppermute x3, waiting for transfers between devices: 9.92 us -> 0.01 us  [from_next(): return lax.ppermute(value, 'x', [((i + distance) % 4, i) for i in range(4)])]
    all_to_all x3 -> x2, starting transfers between devices: 18.3 us -> 12.4 us  [exchange(): return lax.all_to_all(parts, axes, 0, 0, tiled=True)]
    ppermute x2, starting transfers between devices: 15.1 us -> 13.9 us  [swap_cores(): return lax.ppermute(value, 'core', ((0, 1), (1, 0)))]
    all_to_all x3 -> x2, waiting for transfers between devices: 10.3 us -> 9.74 us  [exchange(): return lax.all_to_all(parts, axes, 0, 0, tiled=True)]
  transfers between devices with their start and end apart: 8 -> 7, of which waited for: 6 -> 4; matrix products, arithmetic and copies ran while one was open for 1% -> 0% of each run, Pallas kernels for 1% -> 5%
where the time goes in v9:
time: 100 us; the launch traced here: 99.7 us
  starting transfers between devices  35.6 us (36%)
  blocking collectives  34.5 us (34%)
  Pallas kernels  13.9 us (14%)
  waiting for transfers between devices  11.7 us (12%)
  local copies, waits for them, and re-layouts  2.01 us (2%)
  other arithmetic  1.06 us (1%)
    all_to_all x2, blocking collectives, exchange(): return lax.all_to_all(parts, axes, 0, 0, tiled=True)  34.5 us
    ppermute x2, starting transfers between devices, swap_cores(): return lax.ppermute(value, 'core', ((0, 1), (1, 0)))  13.9 us
    all_to_all x2, starting transfers between devices, exchange(): return lax.all_to_all(parts, axes, 0, 0, tiled=True)  12.4 us
    all_to_all x2, waiting for transfers between devices, exchange(): return lax.all_to_all(parts, axes, 0, 0, tiled=True)  9.74 us
    ppermute x3, starting transfers between devices, from_next(): return lax.ppermute(value, 'x', [((i + distance) % 4, i) for i in range(4)])  9.32 us
    pallas_call x1, Pallas kernels, second_turns(): pl.pallas_call(second_kernel, out_shape=(jax.ShapeDtypeStruct((rows, 128)...  7.81 us
    pallas_call x1, Pallas kernels, first_turns(): pl.pallas_call(first_kernel, out_shape=jax.ShapeDtypeStruct((640, 128), j...  3.84 us
  transfers between devices with their start and end apart: 7, of which 4 were waited for; matrix products, arithmetic and copies ran while one was open for 0% of the time, Pallas kernels for 5%

profile of v9, /device:TPU:1, one launch (start us, length us, event | category | flops | bytes accessed | tf_op | source)
XLA Modules:
  0.0 99.7 jit_solution(12622553085519942522)
XLA Ops:
  0.6 5.0 %all-to-all-start = ((f32[4,512,128]{2,1,0:T(8,128)}), f32[4,512,128]{2,1,0:T(8,128)S(1)}, u32[]{:S(2)}, u32[]{:S(2)}) async-start(f32[4,512,128]{2,1,0:T(8,128)} %bitcast.6), calls=%async_computation | async-start | bytes 2097152 | tf_op jit(solution)/shard_map/all_to_all | solution.py:337
  5.6 0.1 pad_add_fusion.place_ref
  5.7 0.8 shard_map.41
  6.5 0.9 copy-done.3
  7.5 0.9 copy-done.5
  8.3 7.0 %all-to-all-done.m_ref.blocks_ref = f32[4,512,128]{2,1,0:T(8,128)S(1)} async-done(((f32[4,512,128]{2,1,0:T(8,128)}), f32[4,512,128]{2,1,0:T(8,128)S(1)}, u32[]{:S(2)}, u32[]{:S(2)}) %all-to-all-start) | async-done | bytes 1048608 | tf_op jit(solution)/shard_map/all_to_all | solution.py:337
  15.4 1.1 %shard_map.42 = (f32[544,128]{1,0:T(8,128)S(1)}, f32[544,128]{1,0:T(8,128)S(1)}) custom-call(s32[1]{0:T(128)} %bitcast.core_ref, f32[4,512,128]{2,1,0:T(8,128)S(1)} %all-to-all-done.m_ref.blocks_ref), custom_call_target="tpu_custom_call" | custom-call | tf_op jit(solution)/shard_map/pallas_call | solution.py:327
  16.4 8.7 %collective-permute-start = (f32[544,128]{1,0:T(8,128)S(1)}, f32[544,128]{1,0:T(8,128)S(1)}, u32[]{:S(2)}, u32[]{:S(2)}) collective-permute-start(f32[544,128]{1,0:T(8,128)S(1)} %get-tuple-element.31), channel_id=1, source_target_pairs={{0,4},{4,0},{1,5},{5,1},{2,6},{6,2},{3,7},{7,3},{8,12},{12,8},{9,1... | collective-permute-start | bytes 835592 | tf_op jit(solution)/shard_map/ppermute | solution.py:350
  25.2 0.4 shard_map.43
  25.6 0.8 collective-permute-done
  26.3 0.8 add.3
  27.1 7.5 %all-to-all-start.1 = ((f32[32,1,2176]{2,1,0:T(1,128)}), f32[32,1,2176]{2,1,0:T(1,128)S(1)}, u32[]{:S(2)}, u32[]{:S(2)}) async-start(f32[32,1,2176]{2,1,0:T(1,128)} %bitcast.8), calls=%async_computation.1 | async-start | bytes 557056 | tf_op jit(solution)/shard_map/all_to_all | solution.py:337
  34.5 4.3 %collective-permute-start.1 = (f32[1536,128]{1,0:T(8,128)}, f32[1536,128]{1,0:T(8,128)S(1)}, u32[]{:S(2)}, u32[]{:S(2)}) collective-permute-start(f32[1536,128]{1,0:T(8,128)} %copy-done.5), channel_id=1, source_target_pairs={{1,0},{2,1},{3,2},{0,3},{5,4},{6,5},{7,6},{4,7},{9,8},{10,9},{11,1... | collective-permute-start | bytes 2359304 | tf_op jit(solution)/shard_map/ppermute | solution.py:354
  38.9 2.5 %collective-permute-start.2 = (f32[1536,128]{1,0:T(8,128)S(1)}, f32[1536,128]{1,0:T(8,128)}, u32[]{:S(2)}, u32[]{:S(2)}) collective-permute-start(f32[1536,128]{1,0:T(8,128)S(1)} %copy-done.4), channel_id=1, source_target_pairs={{2,0},{3,1},{0,2},{1,3},{6,4},{7,5},{4,6},{5,7},{10,8},{11,9},{8,1... | collective-permute-start | bytes 2359304 | tf_op jit(solution)/shard_map/ppermute | solution.py:354
  41.4 2.5 %collective-permute-start.3 = (f32[1536,128]{1,0:T(8,128)S(1)}, f32[1536,128]{1,0:T(8,128)}, u32[]{:S(2)}, u32[]{:S(2)}) collective-permute-start(f32[1536,128]{1,0:T(8,128)S(1)} %get-tuple-element.45), channel_id=1, source_target_pairs={{3,0},{0,1},{1,2},{2,3},{7,4},{4,5},{5,6},{6,7},{11,8},{8,9},{9,10... | collective-permute-start | bytes 2359304 | tf_op jit(solution)/shard_map/ppermute | solution.py:354
  43.9 2.7 %all-to-all-done.1 = f32[32,1,2176]{2,1,0:T(1,128)S(1)} async-done(((f32[32,1,2176]{2,1,0:T(1,128)}), f32[32,1,2176]{2,1,0:T(1,128)S(1)}, u32[]{:S(2)}, u32[]{:S(2)}) %all-to-all-start.1) | async-done | bytes 278560 | tf_op jit(solution)/shard_map/all_to_all | solution.py:337
  46.6 0.2 reduce_sum.18
  46.8 17.1 %all_to_all.20 = f32[8,1,2176]{2,1,0:T(1,128)S(1)} all-to-all(f32[8,1,2176]{2,1,0:T(1,128)S(1)} %broadcast_in_dim.4), channel_id=1, replica_groups=mesh['z'=8,'y'=8,'core'=2,'x'=4] {'z'}, dimensions={0} | all-to-all | bytes 139264 | tf_op jit(solution)/shard_map/all_to_all | solution.py:337
  64.0 0.1 broadcast_in_dim.5
  64.2 17.4 %all_to_all.21 = f32[32,1,2176]{2,1,0:T(1,128)S(1)} all-to-all(f32[32,1,2176]{2,1,0:T(1,128)S(1)} %broadcast_in_dim.5), channel_id=1, replica_groups=mesh['z'=8,'y'=8,'core'=2,'x'=4] {'y','x'}, dimensions={0} | all-to-all | bytes 557056 | tf_op jit(solution)/shard_map/all_to_all | solution.py:337
  81.6 3.8 %shard_map.44.own_ref = f32[640,128]{1,0:T(8,128)S(1)} custom-call(s32[2]{0:T(128)S(1)} %pad_add_fusion.place_ref, f32[544,128]{1,0:T(8,128)S(1)} %bitcast.7, bf16[2,256,256]{2,1,0:T(8,128)(2,1)S(1)} %get-tuple-element.41.start_ref, bf16[2,256,256]{2,1,0:T(8,128)(2,1)S(1)} %get-tuple-element.42.end_ref), custom_call_target="tpu_custom_call" | custom-call | tf_op jit(solution)/shard_map/pallas_call | solution.py:172
  85.5 5.2 %collective-permute-start.4 = (f32[640,128]{1,0:T(8,128)S(1)}, f32[640,128]{1,0:T(8,128)S(1)}, u32[]{:S(2)}, u32[]{:S(2)}) collective-permute-start(f32[640,128]{1,0:T(8,128)S(1)} %shard_map.44.own_ref), channel_id=1, source_target_pairs={{0,4},{4,0},{1,5},{5,1},{2,6},{6,2},{3,7},{7,3},{8,12},{12,8},{9,1... | collective-permute-start | bytes 983048 | tf_op jit(solution)/shard_map/ppermute | solution.py:350
  90.6 1.2 %collective-permute-done.4.other_ref = f32[640,128]{1,0:T(8,128)S(1)} collective-permute-done((f32[640,128]{1,0:T(8,128)S(1)}, f32[640,128]{1,0:T(8,128)S(1)}, u32[]{:S(2)}, u32[]{:S(2)}) %collective-permute-start.4) | collective-permute-done | bytes 327712 | tf_op jit(solution)/shard_map/ppermute | solution.py:350
  91.8 7.8 %shard_map.45 = (f32[2048,128]{1,0:T(8,128)}, f32[1,128]{1,0:T(1,128)}) custom-call(s32[2]{0:T(128)S(1)} %pad_add_fusion.place_ref, f32[640,128]{1,0:T(8,128)S(1)} %shard_map.44.own_ref, f32[640,128]{1,0:T(8,128)S(1)} %collective-permute-done.4.other_ref, bf16[2,256,256]{2,1,0:T(8,128)(2,1)S(1)} %get-tuple-element.41.start_ref, ...), custom_call_target="tpu_custom_call" | custom-call | tf_op jit(solution)/shard_map/pallas_call | solution.py:237
  (15 shorter events, 0.1 us)
Async XLA Ops:
  0.6 5.1 %copy-start = (f32[2048,128]{1,0:T(8,128)S(1)}, f32[2048,128]{1,0:T(8,128)}, u32[]{:S(2)}) copy-start(f32[2048,128]{1,0:T(8,128)} %matrix_ref.1) | copy-start | bytes 3145732
  0.6 14.7 %all-to-all-start = ((f32[4,512,128]{2,1,0:T(8,128)}), f32[4,512,128]{2,1,0:T(8,128)S(1)}, u32[]{:S(2)}, u32[]{:S(2)}) async-start(f32[4,512,128]{2,1,0:T(8,128)} %bitcast.6), calls=%async_computation | async-start | bytes 2097152 | tf_op jit(solution)/shard_map/all_to_all | solution.py:337
  6.5 0.9 copy-start.3
  7.5 0.9 copy-start.5
  15.4 11.7 %copy-start.1 = (f32[4,512,128]{2,1,0:T(8,128)}, f32[4,512,128]{2,1,0:T(8,128)S(1)}, u32[]{:S(2)}) copy-start(f32[4,512,128]{2,1,0:T(8,128)S(1)} %all-to-all-done.m_ref.blocks_ref) | copy-start | bytes 3145732
  15.4 9.8 %copy-start.2 = (s32[2,256]{1,0:T(2,128)S(1)}, s32[2,256]{1,0:T(2,128)}, u32[]{:S(2)}) copy-start(s32[2,256]{1,0:T(2,128)} %order_ref.1) | copy-start | bytes 6148
  16.4 22.5 %copy-start.4 = (f32[1536,128]{1,0:T(8,128)S(1)}, f32[1536,128]{1,0:T(8,128)}, u32[]{:S(2)}) copy-start(f32[1536,128]{1,0:T(8,128)} %copy-done.3) | copy-start | bytes 2359300
  16.4 9.9 %collective-permute-start = (f32[544,128]{1,0:T(8,128)S(1)}, f32[544,128]{1,0:T(8,128)S(1)}, u32[]{:S(2)}, u32[]{:S(2)}) collective-permute-start(f32[544,128]{1,0:T(8,128)S(1)} %get-tuple-element.31), channel_id=1, source_target_pairs={{0,4},{4,0},{1,5},{5,1},{2,6},{6,2},{3,7},{7,3},{8,12},{12,8},{9,1... | collective-permute-start | bytes 835592 | tf_op jit(solution)/shard_map/ppermute | solution.py:350
  27.1 19.5 %all-to-all-start.1 = ((f32[32,1,2176]{2,1,0:T(1,128)}), f32[32,1,2176]{2,1,0:T(1,128)S(1)}, u32[]{:S(2)}, u32[]{:S(2)}) async-start(f32[32,1,2176]{2,1,0:T(1,128)} %bitcast.8), calls=%async_computation.1 | async-start | bytes 557056 | tf_op jit(solution)/shard_map/all_to_all | solution.py:337
  34.5 50.9 %collective-permute-start.1 = (f32[1536,128]{1,0:T(8,128)}, f32[1536,128]{1,0:T(8,128)S(1)}, u32[]{:S(2)}, u32[]{:S(2)}) collective-permute-start(f32[1536,128]{1,0:T(8,128)} %copy-done.5), channel_id=1, source_target_pairs={{1,0},{2,1},{3,2},{0,3},{5,4},{6,5},{7,6},{4,7},{9,8},{10,9},{11,1... | collective-permute-start | bytes 2359304 | tf_op jit(solution)/shard_map/ppermute | solution.py:354
  38.9 46.5 %collective-permute-start.2 = (f32[1536,128]{1,0:T(8,128)S(1)}, f32[1536,128]{1,0:T(8,128)}, u32[]{:S(2)}, u32[]{:S(2)}) collective-permute-start(f32[1536,128]{1,0:T(8,128)S(1)} %copy-done.4), channel_id=1, source_target_pairs={{2,0},{3,1},{0,2},{1,3},{6,4},{7,5},{4,6},{5,7},{10,8},{11,9},{8,1... | collective-permute-start | bytes 2359304 | tf_op jit(solution)/shard_map/ppermute | solution.py:354
  41.4 44.0 %collective-permute-start.3 = (f32[1536,128]{1,0:T(8,128)S(1)}, f32[1536,128]{1,0:T(8,128)}, u32[]{:S(2)}, u32[]{:S(2)}) collective-permute-start(f32[1536,128]{1,0:T(8,128)S(1)} %get-tuple-element.45), channel_id=1, source_target_pairs={{3,0},{0,1},{1,2},{2,3},{7,4},{4,5},{5,6},{6,7},{11,8},{8,9},{9,10... | collective-permute-start | bytes 2359304 | tf_op jit(solution)/shard_map/ppermute | solution.py:354
  85.5 6.4 %collective-permute-start.4 = (f32[640,128]{1,0:T(8,128)S(1)}, f32[640,128]{1,0:T(8,128)S(1)}, u32[]{:S(2)}, u32[]{:S(2)}) collective-permute-start(f32[640,128]{1,0:T(8,128)S(1)} %shard_map.44.own_ref), channel_id=1, source_target_pairs={{0,4},{4,0},{1,5},{5,1},{2,6},{6,2},{3,7},{7,3},{8,12},{12,8},{9,1... | collective-permute-start | bytes 983048 | tf_op jit(solution)/shard_map/ppermute | solution.py:350
